TPU v7x, 32 devices: a whole 2x2x4 slice. The times are simulated.
32 devices in a mesh: groups: 2 (over y), dp: 4 (over z), mp: 4 (over x, core).
Axes of the slice: x: 2, y: 2, z: 4, core: 2. Of those that a mesh axis runs over, the one named last changes fastest.
Arguments:
- replay: bfloat16 [8192, 1024], P(('groups', 'dp'), 'mp'), parts along dimension 0, may hold values from -17 to 17
- sa_row: int32 [1024], P(('groups', 'dp')), parts along dimension 0, may hold values from 0 to 1023
- goal_owner: int32 [1024, 1], P(('groups', 'dp')), parts along dimension 0, may hold values from 0 to 3; in each aligned block of 128 rows (0 to 127, 128 to 255, ...) at most 64 rows name the same one
- goal_row: int32 [1024], P(('groups', 'dp')), parts along dimension 0, may hold values from 0 to 1023
- state_first: bfloat16 [1024, 2048], P(None, 'mp'), may hold values from -0.1875 to 0.1875
- state_second: bfloat16 [2048, 1024], P('mp'), may hold values from -0.125 to 0.125
- goal_first: bfloat16 [1024, 2048], P(None, 'mp'), may hold values from -0.1875 to 0.1875
- goal_second: bfloat16 [2048, 1024], P('mp'), may hold values from -0.125 to 0.125
Outputs:
- state_first_grad: float32 [2048, 2048], P(('groups', 'dp'), 'mp'), parts along dimension 0
- state_second_grad: float32 [4096, 1024], P(('groups', 'mp'), 'dp'), parts along dimension 0
- goal_first_grad: float32 [2048, 2048], P(('groups', 'dp'), 'mp'), parts along dimension 0
- goal_second_grad: float32 [4096, 1024], P(('groups', 'mp'), 'dp'), parts along dimension 0
There are 2 independent parts, one for each index of `groups`. A program takes and returns all parts, laid end to end along the dimension named above; an argument that names none is the same for every part. Nothing has to cross between parts.
Inputs may be any that keep to these rules, and one draw needn't show every extreme that they name: `goal_owner`: within the 128 rows of one device no owner is named more than 64 times, and in every draw some owner is named exactly 64 times by the rows of some device.
All inputs are finite; a program needn't handle non-finite values.
Results may differ from a plain program's by a relative error of at most 0.01615.
Values may be sent and summed in bfloat16 or wider, within the bound.
No kernel may reach another device: no remote copies, remote signals or barrier semaphores. Data moves between devices by JAX's collectives and lax.ppermute only.
A program may use at most 64 MiB of HBM per device.

v0:
```python
import math

import jax
import jax.numpy as jnp
from jax import lax
from jax.sharding import PartitionSpec as P


def silu_slope(value):
    sig = jax.nn.sigmoid(value)
    return sig * (1.0 + value * (1.0 - sig))


def slot_numbers(owner_list, shards):
    hits = (owner_list[:, None] == jnp.arange(shards, dtype=jnp.int32)[None, :]).astype(jnp.int32)
    before = jnp.cumsum(hits, axis=0) - hits
    return jnp.sum(before * hits, axis=1)


def local_terms(latent, pre, act, grad, second):
    second_term = jnp.einsum("ru,re->ue", act, grad, preferred_element_type=jnp.float32)
    back = jnp.einsum("re,ue->ru", grad, second, preferred_element_type=jnp.float32)
    slope = (back * silu_slope(pre)).astype(jnp.bfloat16)
    first_term = jnp.einsum("rl,ru->lu", latent, slope, preferred_element_type=jnp.float32)
    return (first_term, second_term)


def body(replay, sa_row, goal_owner, goal_row, state_first, state_second, goal_first, goal_second):
    shards = lax.axis_size("dp")
    models = lax.axis_size("mp")
    here = lax.axis_index("dp")
    group = lax.axis_index("mp")
    rows = sa_row.shape[0]
    slots = 2 * rows // shards
    share = rows // models
    width = replay.shape[1]
    owners = goal_owner[:, 0]
    state_local = jnp.take(replay, sa_row, axis=0)
    position = owners * slots + slot_numbers(owners, shards)
    places = jnp.arange(shards * slots, dtype=jnp.int32)
    chosen = position[None, :] == places[:, None]
    requests = jnp.sum(jnp.where(chosen, goal_row[None, :], 0), axis=1).reshape(shards, slots)
    found = jnp.take(
        replay, lax.all_to_all(requests, "dp", split_axis=0, concat_axis=0, tiled=True), axis=0
    )
    returned = lax.all_to_all(found, "dp", split_axis=0, concat_axis=0, tiled=True)
    goal_local = jnp.take(returned.reshape(shards * slots, width), position, axis=0)
    state_x, goal_x = (
        lax.all_gather(state_local, "mp", axis=1, tiled=True),
        lax.all_gather(goal_local, "mp", axis=1, tiled=True),
    )
    state_pre = jnp.dot(state_x, state_first, preferred_element_type=jnp.float32)
    state_act = jax.nn.silu(state_pre).astype(jnp.bfloat16)
    state_part = jnp.dot(state_act, state_second, preferred_element_type=jnp.float32)
    goal_pre = jnp.dot(goal_x, goal_first, preferred_element_type=jnp.float32)
    goal_act = jax.nn.silu(goal_pre).astype(jnp.bfloat16)
    goal_part = jnp.dot(goal_act, goal_second, preferred_element_type=jnp.float32)
    state_total, goal_total = lax.psum((state_part, goal_part), "mp")
    phi = state_total.astype(jnp.bfloat16)
    psi_mine = lax.dynamic_slice_in_dim(goal_total, group * share, share, 0).astype(jnp.bfloat16)
    psi_cols = lax.all_gather(psi_mine, "dp", axis=0, tiled=True)
    scale = 4.0 / math.sqrt(phi.shape[1])
    scores = scale * jnp.einsum("re,ce->rc", phi, psi_cols, preferred_element_type=jnp.float32)
    local_top = jnp.max(scores, axis=1)
    top = lax.pmax(local_top, "mp")
    total = lax.psum(jnp.sum(jnp.exp(scores - top[:, None]), axis=1), "mp")
    lse = top + jnp.log(total)
    row_ids = jnp.arange(rows, dtype=jnp.int32)[:, None]
    col_ids = jnp.arange(scores.shape[1], dtype=jnp.int32)[None, :]
    target = here * share + row_ids - group * share
    positive = (row_ids // share == group) & (col_ids == target)
    weights = (jnp.exp(scores - lse[:, None]) - positive.astype(jnp.float32)).astype(jnp.bfloat16)
    row_part = scale * jnp.einsum(
        "rc,ce->re", weights, psi_cols, preferred_element_type=jnp.float32
    )
    phi_grad = lax.psum(row_part.astype(jnp.bfloat16), "mp")
    psi_grad_mine = lax.psum_scatter(
        (scale * jnp.einsum("rc,re->ce", weights, phi, preferred_element_type=jnp.float32)).astype(
            jnp.bfloat16
        ),
        "dp",
        scatter_dimension=0,
        tiled=True,
    )
    psi_grad = lax.all_gather(psi_grad_mine, "mp", axis=0, tiled=True)
    state_one, state_two = local_terms(state_x, state_pre, state_act, phi_grad, state_second)
    goal_one, goal_two = local_terms(goal_x, goal_pre, goal_act, psi_grad, goal_second)
    grads = (
        lax.psum_scatter(
            state_one.astype(jnp.bfloat16), "dp", scatter_dimension=0, tiled=True
        ).astype(jnp.float32),
        lax.psum_scatter(
            state_two.astype(jnp.bfloat16), "dp", scatter_dimension=1, tiled=True
        ).astype(jnp.float32),
        lax.psum_scatter(
            goal_one.astype(jnp.bfloat16), "dp", scatter_dimension=0, tiled=True
        ).astype(jnp.float32),
        lax.psum_scatter(
            goal_two.astype(jnp.bfloat16), "dp", scatter_dimension=1, tiled=True
        ).astype(jnp.float32),
    )
    return (grads[0], grads[1], grads[2], grads[3])


def solution(mesh):
    in_specs = (
        P(("groups", "dp"), "mp"),
        P(("groups", "dp")),
        P(("groups", "dp"), None),
        P(("groups", "dp")),
        P(None, "mp"),
        P("mp", None),
        P(None, "mp"),
        P("mp", None),
    )
    out_specs = (
        P(("groups", "dp"), "mp"),
        P(("groups", "mp"), "dp"),
        P(("groups", "dp"), "mp"),
        P(("groups", "mp"), "dp"),
    )
    return jax.shard_map(body, mesh=mesh, in_specs=in_specs, out_specs=out_specs, check_vma=False)
```

profile of v0, /device:TPU:0, one launch (start us, length us, event | category | flops | bytes accessed | tf_op | source)
XLA Modules:
  0.0 259.4 jit_solution(17223243912695012577)
XLA Ops:
  8.0 0.0 copy-start
  8.0 0.9 fusion.16
  8.9 0.2 reduce_window_sum.11
  9.1 0.8 select_reduce_fusion.1
  9.9 0.7 multiply_add_fusion
  10.6 0.8 select_reduce_fusion
  11.4 0.7 all_to_all.13
  12.0 6.3 %all-to-all-start = ((s32[4,1,64]{2,1,0:T(1,128)}), s32[4,1,64]{2,1,0:T(1,128)S(1)}, u32[]{:S(2)}, u32[]{:S(2)}) async-start(s32[4,1,64]{2,1,0:T(1,128)} %all_to_all.13), calls=%async_computation | async-start | bytes 4096 | tf_op jit(solution)/shard_map/all_to_all | solution.py:44
  18.3 0.7 compare_and_fusion.1
  19.0 0.7 compare_select_fusion.3
  19.7 0.7 and_bitcast_fusion
  20.3 1.9 gather_fusion
  22.2 0.1 broadcast_select_fusion.2
  22.3 5.8 %all_gather.12 = bf16[128,1024]{1,0:T(8,128)(2,1)S(1)} all-gather(bf16[128,256]{1,0:T(8,128)(2,1)S(1)} %broadcast_select_fusion.2), channel_id=1, replica_groups=mesh['groups'=2,'dp'=4,'mp'=4] {'mp'}, dimensions={1}, use_global_device_ids=true | all-gather | bytes 327680 | tf_op jit(solution)/shard_map/all_gather | solution.py:49
  28.1 0.3 fusion.24
  28.4 0.0 copy-start.1
  28.4 0.3 fusion.21
  28.8 0.1 reshape.128
  28.9 0.6 copy-done.1
  29.4 1.1 gather_fusion.1
  30.6 0.8 broadcast_select_fusion
  31.4 5.1 %all-to-all-start.1 = ((bf16[4,64,256]{2,1,0:T(8,128)(2,1)}), bf16[4,64,256]{2,1,0:T(8,128)(2,1)S(1)}, u32[]{:S(2)}, u32[]{:S(2)}) async-start(bf16[4,64,256]{2,1,0:T(8,128)(2,1)} %broadcast_select_fusion), calls=%async_computation.1 | async-start | bytes 262144 | tf_op jit(solution)/shard_map/all_to_all | solution.py:46
  36.5 6.4 %all-to-all-done.1 = bf16[4,64,256]{2,1,0:T(8,128)(2,1)S(1)} async-done(((bf16[4,64,256]{2,1,0:T(8,128)(2,1)}), bf16[4,64,256]{2,1,0:T(8,128)(2,1)S(1)}, u32[]{:S(2)}, u32[]{:S(2)}) %all-to-all-start.1) | async-done | bytes 131104 | tf_op jit(solution)/shard_map/all_to_all | solution.py:46
  42.9 0.8 gather_fusion.2
  43.7 0.0 copy-start.6
  43.7 0.1 broadcast_select_fusion.1
  43.8 5.9 %all_gather.13 = bf16[128,1024]{1,0:T(8,128)(2,1)S(1)} all-gather(bf16[128,256]{1,0:T(8,128)(2,1)S(1)} %broadcast_select_fusion.1), channel_id=1, replica_groups=mesh['groups'=2,'dp'=4,'mp'=4] {'mp'}, dimensions={1}, use_global_device_ids=true | all-gather | bytes 327680 | tf_op jit(solution)/shard_map/all_gather | solution.py:50
  49.8 0.3 fusion.25
  50.1 0.7 copy-done.4
  50.8 0.3 fusion.22
  51.1 26.6 %all-reduce.5 = (bf16[128,1024]{1,0:T(8,128)(2,1)S(1)}, bf16[128,1024]{1,0:T(8,128)(2,1)S(1)}) all-reduce(f32[128,1024]{1,0:T(8,128)S(1)} %fusion.22, f32[128,1024]{1,0:T(8,128)S(1)} %fusion.21), channel_id=1, replica_groups=mesh['groups'=2,'dp'=4,'mp'=4] {'mp'}, use_global_device_ids=true, to_apply=%region_4.5 | all-reduce | flops 262144 | bytes 1572864 | tf_op jit(solution)/shard_map/psum | solution.py:58
  77.7 13.8 %all_gather.14 = bf16[128,1024]{1,0:T(8,128)(2,1)S(1)} all-gather(bf16[32,1024]{1,0:T(8,128)(2,1)S(1)} %dynamic-slice_convert_fusion), channel_id=1, replica_groups=mesh['groups'=2,'dp'=4,'mp'=4] {'dp'}, dimensions={0}, use_global_device_ids=true | all-gather | bytes 327680 | tf_op jit(solution)/shard_map/all_gather | solution.py:61
  91.5 0.2 fusion.23
  91.8 5.7 %pmax.7 = f32[128]{0:T(128)S(1)} all-reduce(f32[128]{0:T(128)S(1)} %get-tuple-element.8), channel_id=1, replica_groups=mesh['groups'=2,'dp'=4,'mp'=4] {'mp'}, use_global_device_ids=true, to_apply=%region_6.7 | all-reduce | flops 128 | bytes 1024 | tf_op jit(solution)/shard_map/pmax | solution.py:65
  97.5 6.0 %psum.30 = f32[128]{0:T(128)S(1)} all-reduce(f32[128]{0:T(128)S(1)} %exponential_reduce_fusion), channel_id=1, replica_groups=mesh['groups'=2,'dp'=4,'mp'=4] {'mp'}, use_global_device_ids=true, to_apply=%region_8.9 | all-reduce | flops 128 | bytes 1024 | tf_op jit(solution)/shard_map/psum | solution.py:66
  103.6 1.0 fusion
  104.5 0.0 all-reduce.4.cloned.1.call-update
  104.6 0.0 reduce-scatter.10.cloned.1.call-start
  104.6 0.9 fusion.1
  105.5 0.0 reduce-scatter.10.cloned.1.call-update
  105.6 0.0 reduce-scatter.6.cloned.1.call-start
  105.6 30.1 %all-reduce.4.cloned.1.call-done = bf16[128,1024]{1,0:T(8,128)(2,1)} async-done(((bf16[128,1024]{1,0:T(8,128)(2,1)}), bf16[128,1024]{1,0:T(8,128)(2,1)}) %all-reduce.4.cloned.1.call-update) | async-done | bytes 262160 | tf_op jit(solution)/shard_map/psum | solution.py:76
  135.8 2.8 %convolution_convert_fusion.3 = bf16[1024,512]{1,0:T(8,128)(2,1)} fusion(bf16[128,1024]{1,0:T(8,128)(2,1)S(1)} %all_gather.12, bf16[128,1024]{1,0:T(8,128)(2,1)} %all-reduce.4.cloned.1.call-done, bf16[512,1024]{1,0:T(8,128)(2,1)S(1)} %copy-done, f32[128,512]{1,0:T(8,128)S(1)} %fusion.24), kind=kOutput, calls=%fused_computation.6 | convolution fusion | flops 269549568 | bytes 2883584 | tf_op jit(solution)/shard_map/rl,ru->lu/dot_general | solution.py:24
  138.6 0.0 reduce-scatter.6.cloned.1.call-update
  138.6 0.0 reduce-scatter.8.cloned.1.call-start
  138.7 0.9 copy-done.8
  139.5 1.5 convolution_convert_fusion.2
  141.0 0.0 reduce-scatter.8.cloned.1.call-update
  141.1 0.0 reduce-scatter.12.cloned.1.call-start
  141.1 0.0 reduce-scatter.10.cloned.1.call-done
  141.2 6.1 %all_gather.15 = bf16[128,1024]{1,0:T(8,128)(2,1)S(1)} all-gather(bf16[32,1024]{1,0:T(8,128)(2,1)} %reduce-scatter.10.cloned.1.call-done), channel_id=1, replica_groups=mesh['groups'=2,'dp'=4,'mp'=4] {'mp'}, dimensions={0}, use_global_device_ids=true | all-gather | bytes 327680 | tf_op jit(solution)/shard_map/all_gather | solution.py:85
  147.3 1.9 convolution_convert_fusion.1
  149.2 0.0 reduce-scatter.12.cloned.1.call-update
  149.2 0.0 reduce-scatter.14.cloned.1.call-start
  149.2 1.5 convolution_convert_fusion
  150.7 0.0 reduce-scatter.14.cloned.1.call-update
  150.7 15.1 %reduce-scatter.6.cloned.1.call-done = bf16[256,512]{1,0:T(8,128)(2,1)} async-done(((bf16[1024,512]{1,0:T(8,128)(2,1)}), bf16[256,512]{1,0:T(8,128)(2,1)}) %reduce-scatter.6.cloned.1.call-update) | async-done | bytes 262160 | tf_op jit(solution)/shard_map/reduce_scatter | solution.py:89
  165.9 1.8 convert_element_type.67
  167.7 26.2 %reduce-scatter.8.cloned.1.call-done = bf16[512,256]{1,0:T(8,128)(2,1)} async-done(((bf16[512,1024]{1,0:T(8,128)(2,1)}), bf16[512,256]{1,0:T(8,128)(2,1)}) %reduce-scatter.8.cloned.1.call-update) | async-done | bytes 262160 | tf_op jit(solution)/shard_map/reduce_scatter | solution.py:92
  193.9 1.8 convert_element_type.69
  195.6 26.3 %reduce-scatter.12.cloned.1.call-done = bf16[256,512]{1,0:T(8,128)(2,1)} async-done(((bf16[1024,512]{1,0:T(8,128)(2,1)}), bf16[256,512]{1,0:T(8,128)(2,1)}) %reduce-scatter.12.cloned.1.call-update) | async-done | bytes 262160 | tf_op jit(solution)/shard_map/reduce_scatter | solution.py:95
  221.9 1.8 convert_element_type.73
  223.7 26.3 %reduce-scatter.14.cloned.1.call-done = bf16[512,256]{1,0:T(8,128)(2,1)} async-done(((bf16[512,1024]{1,0:T(8,128)(2,1)}), bf16[512,256]{1,0:T(8,128)(2,1)}) %reduce-scatter.14.cloned.1.call-update) | async-done | bytes 262160 | tf_op jit(solution)/shard_map/reduce_scatter | solution.py:98
  250.1 1.8 convert_element_type.75
  (24 shorter events, 0.1 us)
Async XLA Ops:
  8.0 20.4 %copy-start = (bf16[512,1024]{1,0:T(8,128)(2,1)S(1)}, bf16[512,1024]{1,0:T(8,128)(2,1)}, u32[]{:S(2)}) copy-start(bf16[512,1024]{1,0:T(8,128)(2,1)} %param.13) | copy-start | bytes 3145732
  8.0 20.1 %copy-start.2 = (bf16[1024,512]{1,0:T(8,128)(2,1)S(1)}, bf16[1024,512]{1,0:T(8,128)(2,1)}, u32[]{:S(2)}) copy-start(bf16[1024,512]{1,0:T(8,128)(2,1)} %param.12) | copy-start | bytes 3145732
  12.0 16.7 %all-to-all-start = ((s32[4,1,64]{2,1,0:T(1,128)}), s32[4,1,64]{2,1,0:T(1,128)S(1)}, u32[]{:S(2)}, u32[]{:S(2)}) async-start(s32[4,1,64]{2,1,0:T(1,128)} %all_to_all.13), calls=%async_computation | async-start | bytes 4096 | tf_op jit(solution)/shard_map/all_to_all | solution.py:44
  28.4 1.0 copy-start.1
  30.6 19.2 %copy-start.3 = (bf16[1024,512]{1,0:T(8,128)(2,1)S(1)}, bf16[1024,512]{1,0:T(8,128)(2,1)}, u32[]{:S(2)}) copy-start(bf16[1024,512]{1,0:T(8,128)(2,1)} %param.14) | copy-start | bytes 3145732
  31.4 11.5 %all-to-all-start.1 = ((bf16[4,64,256]{2,1,0:T(8,128)(2,1)}), bf16[4,64,256]{2,1,0:T(8,128)(2,1)S(1)}, u32[]{:S(2)}, u32[]{:S(2)}) async-start(bf16[4,64,256]{2,1,0:T(8,128)(2,1)} %broadcast_select_fusion), calls=%async_computation.1 | async-start | bytes 262144 | tf_op jit(solution)/shard_map/all_to_all | solution.py:46
  36.5 99.3 %all-reduce.4.cloned.1.call-start = ((), (), s32[]{:S(2)}) async-start(), calls=%async_computation.7 | async-start | bytes 524288 | tf_op jit(solution)/shard_map/psum | solution.py:76
  43.7 7.0 %copy-start.6 = (bf16[512,1024]{1,0:T(8,128)(2,1)S(1)}, bf16[512,1024]{1,0:T(8,128)(2,1)}, u32[]{:S(2)}) copy-start(bf16[512,1024]{1,0:T(8,128)(2,1)} %param.15) | copy-start | bytes 3145732
  50.1 0.7 copy-start.4
  104.6 36.6 %reduce-scatter.10.cloned.1.call-start = ((), (), s32[]{:S(2)}) async-start(), calls=%async_computation.10 | async-start | bytes 327680 | tf_op jit(solution)/shard_map/reduce_scatter | solution.py:77
  105.6 60.3 %reduce-scatter.6.cloned.1.call-start = ((), (), s32[]{:S(2)}) async-start(), calls=%async_computation.8 | async-start | bytes 1310720 | tf_op jit(solution)/shard_map/reduce_scatter | solution.py:89
  138.6 0.9 copy-start.8
  138.6 55.2 %reduce-scatter.8.cloned.1.call-start = ((), (), s32[]{:S(2)}) async-start(), calls=%async_computation.9 | async-start | bytes 1310720 | tf_op jit(solution)/shard_map/reduce_scatter | solution.py:92
  141.0 6.2 %copy-start.5 = (f32[128,512]{1,0:T(8,128)S(1)}, f32[128,512]{1,0:T(8,128)}, u32[]{:S(2)}) copy-start(f32[128,512]{1,0:T(8,128)} %copy-done.4) | copy-start | bytes 786436
  141.0 6.2 %copy-start.7 = (bf16[512,1024]{1,0:T(8,128)(2,1)S(1)}, bf16[512,1024]{1,0:T(8,128)(2,1)}, u32[]{:S(2)}) copy-start(bf16[512,1024]{1,0:T(8,128)(2,1)} %param.15) | copy-start | bytes 3145732
  141.1 80.9 %reduce-scatter.12.cloned.1.call-start = ((), (), s32[]{:S(2)}) async-start(), calls=%async_computation.11 | async-start | bytes 1310720 | tf_op jit(solution)/shard_map/reduce_scatter | solution.py:95
  149.2 100.9 %reduce-scatter.14.cloned.1.call-start = ((), (), s32[]{:S(2)}) async-start(), calls=%async_computation.12 | async-start | bytes 1310720 | tf_op jit(solution)/shard_map/reduce_scatter | solution.py:98
Sparse Core Ops, SparseCore 0:
  104.7 31.0 all-reduce.3
Sparse Core Ops, SparseCore 1:
  107.9 18.8 reduce-scatter.9
  138.7 27.1 reduce-scatter.5
  168.1 25.7 reduce-scatter.7
  196.2 25.7 reduce-scatter.11
  224.3 25.7 reduce-scatter.13
where the time goes:
time: 260 us; the launch traced here: 259 us
  waiting for transfers between devices  131 us (50%)
  blocking collectives  70 us (27%)
  between operations  15.9 us (6%)
  other arithmetic  13.5 us (5%)
  starting transfers between devices  11.6 us (4%)
  matrix products  11.1 us (4%)
  local copies, waits for them, and re-layouts  6.8 us (3%)
    psum x1, waiting for transfers between devices, body(): phi_grad = lax.psum(row_part.astype(jnp.bfloat16), 'mp')  30.1 us
    psum x1, blocking collectives, body(): state_total, goal_total = lax.psum((state_part, goal_part), 'mp')  26.6 us
    reduce_scatter x1, waiting for transfers between devices, body(): lax.psum_scatter(goal_two.astype(jnp.bfloat16), 'dp', scatter_dimension=1...  26.3 us
    reduce_scatter x1, waiting for transfers between devices, body(): lax.psum_scatter(goal_one.astype(jnp.bfloat16), 'dp', scatter_dimension=0...  26.3 us
    reduce_scatter x1, waiting for transfers between devices, body(): lax.psum_scatter(state_two.astype(jnp.bfloat16), 'dp', scatter_dimension=...  26.2 us
    reduce_scatter x1, waiting for transfers between devices, body(): lax.psum_scatter(state_one.astype(jnp.bfloat16), 'dp', scatter_dimension=...  15.1 us
    all_gather x1, blocking collectives, body(): psi_cols = lax.all_gather(psi_mine, 'dp', axis=0, tiled=True)  13.8 us
    convert_element_type x4, other arithmetic, body(): grads = (lax.psum_scatter(state_one.astype(jnp.bfloat16), 'dp', scatter_d...  7.16 us
  transfers between devices with their start and end apart: 8, of which 6 were waited for; matrix products, arithmetic and copies ran while one was open for 7% of the time, Pallas kernels for 0%

commit v1 on v0

--- a/solution.py
+++ b/solution.py
@@ -1,8 +1,11 @@
+import functools
 import math
 
 import jax
 import jax.numpy as jnp
 from jax import lax
+from jax.experimental import pallas as pl
+from jax.experimental.pallas import tpu as pltpu
 from jax.sharding import PartitionSpec as P
 
 
@@ -25,7 +28,7 @@
     return (first_term, second_term)
 
 
-def body(replay, sa_row, goal_owner, goal_row, state_first, state_second, goal_first, goal_second):
+def split_batch(replay, sa_row, goal_owner, goal_row, state_first, state_second, goal_first, goal_second):
     shards = lax.axis_size("dp")
     models = lax.axis_size("mp")
     here = lax.axis_index("dp")
@@ -102,6 +105,305 @@
     return (grads[0], grads[1], grads[2], grads[3])
 
 
+F32 = jnp.float32
+BF16 = jnp.bfloat16
+
+
+def call(kernel, outs, operands, scalars=0, scratch=(), limit=48, flops=0):
+    smem = pl.BlockSpec(memory_space=pltpu.SMEM)
+    vmem = pl.BlockSpec(memory_space=pltpu.VMEM)
+    in_specs = [smem] * scalars + [vmem] * (len(operands) - scalars)
+    moved = sum(a.size * a.dtype.itemsize for a in operands)
+    moved += sum(math.prod(s) * jnp.dtype(d).itemsize for s, d in outs)
+    return pl.pallas_call(
+        kernel,
+        out_shape=[jax.ShapeDtypeStruct(s, d) for s, d in outs],
+        in_specs=in_specs,
+        out_specs=[vmem] * len(outs),
+        scratch_shapes=list(scratch),
+        compiler_params=pltpu.CompilerParams(vmem_limit_bytes=limit * 2**20),
+        cost_estimate=pl.CostEstimate(flops=flops, bytes_accessed=moved, transcendentals=0),
+    )(*operands)
+
+
+def dot(a, b, dims=((1,), (0,))):
+    return lax.dot_general(a, b, (dims, ((), ())), preferred_element_type=F32)
+
+
+def below(rows):
+    earlier = lax.broadcasted_iota(jnp.int32, (rows, rows), 0)
+    later = lax.broadcasted_iota(jnp.int32, (rows, rows), 1)
+    return (earlier < later).astype(F32).astype(BF16)
+
+
+def one_hot(column, width):
+    lanes = lax.broadcasted_iota(jnp.int32, (column.shape[0], width), 1)
+    return (column == lanes).astype(F32).astype(BF16)
+
+
+def pick_kernel(row_ref, replay_ref, out_ref):
+    rows = row_ref.shape[1]
+    wide = jnp.broadcast_to(row_ref[...].astype(F32), (8, rows))
+    column = wide.T[:, 0:1].astype(jnp.int32)
+    out_ref[...] = dot(one_hot(column, replay_ref.shape[0]), replay_ref[...]).astype(BF16)
+
+
+def found_kernel(shards, slots, here_ref, *refs):
+    wants, replay_ref, out_ref, hits_ref = refs[:shards], refs[shards], refs[-2], refs[-1]
+    here = here_ref[0]
+    rows = wants[0].shape[1]
+    hits_ref[...] = jnp.zeros_like(hits_ref)
+    for step in range(shards):
+        hits_ref[step : step + 1, :] = (wants[step][0:1, :] == here).astype(F32)
+    before = dot(hits_ref[...].astype(BF16), below(rows))
+    places = lax.broadcasted_iota(jnp.int32, (slots, rows), 0)
+    for step in range(shards):
+        rank = before[step : step + 1, :].astype(jnp.int32)
+        chosen = (places == rank) & (wants[step][0:1, :] == here)
+        asked = jnp.where(chosen, wants[step][1:2, :].astype(F32), 0.0)
+        column = jnp.sum(asked, axis=1, keepdims=True).astype(jnp.int32)
+        hot = one_hot(column, replay_ref.shape[0])
+        out_ref[step * slots : (step + 1) * slots, :] = dot(hot, replay_ref[...]).astype(BF16)
+
+
+def place_kernel(shards, slots, here_ref, *refs):
+    wants, out_ref, place_ref = refs[:shards], refs[-2], refs[-1]
+    here = here_ref[0]
+    rows = wants[0].shape[1]
+    tri = below(rows)
+    place_ref[...] = jnp.zeros_like(place_ref)
+    owners = lax.broadcasted_iota(jnp.int32, (place_ref.shape[0], rows), 0)
+    for step in range(shards):
+        owner = wants[step][0:1, :]
+        hits = (owners == owner).astype(F32)
+        rank = jnp.sum(dot(hits.astype(BF16), tri) * hits, axis=0, keepdims=True)
+        turn = here - owner
+        turn = jnp.where(turn < 0, turn + shards, turn)
+        block = step - turn
+        block = jnp.where(block < 0, block + shards, block)
+        spot = ((turn * shards + block) * slots).astype(F32) + rank
+        place_ref[step : step + 1, :] = spot
+    out_ref[...] = place_ref[...].T
+
+
+def select_kernel(shards, place_ref, *refs):
+    founds, out_ref = refs[:shards], refs[-1]
+    rows = place_ref.shape[0]
+    size = founds[0].shape[0]
+    for step in range(shards):
+        column = place_ref[:, step : step + 1].astype(jnp.int32)
+        total = dot(one_hot(column, size), founds[0][...])
+        for turn in range(1, shards):
+            total += dot(one_hot(column - turn * size, size), founds[turn][...])
+        out_ref[step * rows : (step + 1) * rows, :] = total.astype(BF16)
+
+
+def hidden(group, pieces, first_ref):
+    width = pieces[0].shape[1]
+    total = None
+    for index, piece in enumerate(pieces):
+        start = pl.multiple_of((group ^ index) * width, width)
+        term = dot(piece[...], first_ref[pl.ds(start, width), :])
+        total = term if total is None else total + term
+    return total
+
+
+def slope_of(value):
+    sig = 1.0 / (1.0 + jnp.exp(-value))
+    return sig * value, sig * (1.0 + value * (1.0 - sig))
+
+
+def part_kernel(group_ref, *refs):
+    pieces, (first_ref, second_ref, keep_ref, send_ref, part_ref) = refs[:4], refs[4:]
+    group = group_ref[0]
+    act, _ = slope_of(hidden(group, pieces, first_ref))
+    part_ref[...] = dot(act.astype(BF16), second_ref[...])
+    half = keep_ref.shape[0]
+    core = group % 2
+    keep_ref[...] = part_ref[pl.ds(pl.multiple_of(core * half, half), half), :]
+    send_ref[...] = part_ref[pl.ds(pl.multiple_of((1 - core) * half, half), half), :]
+
+
+def act_kernel(group_ref, *refs):
+    pieces, (first_ref, act_ref, slope_ref) = refs[:-3], refs[-3:]
+    act, slope = slope_of(hidden(group_ref[0], pieces, first_ref))
+    act_ref[...] = act.astype(BF16)
+    slope_ref[...] = slope
+
+
+def embed_kernel(group_ref, *refs):
+    pieces, firsts, seconds = refs[:4], refs[4:8], refs[8:12]
+    psi_ref, act_ref, slope_ref, total_ref = refs[12:]
+    group = group_ref[0]
+    for index in range(4):
+        act, slope = slope_of(hidden(group, pieces, firsts[index]))
+        act = act.astype(BF16)
+        if index == 0:
+            act_ref[...] = act
+            slope_ref[...] = slope
+        term = dot(act, seconds[index][...])
+        if index == 0:
+            total_ref[...] = term
+        elif index < 3:
+            total_ref[...] += term
+        else:
+            psi_ref[...] = (total_ref[...] + term).astype(BF16)
+
+
+def grads_kernel(shards, group_ref, here_ref, *refs):
+    halves = refs[: 2 * shards]
+    psi_ref, state_x, goal_x = refs[2 * shards], refs[2 * shards + 1 :][:4], refs[2 * shards + 5 :][:4]
+    rest = refs[2 * shards + 9 :]
+    state_act, state_slope, goal_act, goal_slope, state_second, goal_second = rest[:6]
+    outs, (phi_ref, column_ref, grad_ref) = rest[6:10], rest[10:]
+    group, here = group_ref[0], here_ref[0]
+    half = halves[0].shape[0]
+    core = group % 2
+    for step in range(shards):
+        for other in range(2):
+            start = step * 2 * half + (core ^ other) * half
+            phi_ref[pl.ds(pl.multiple_of(start, half), half), :] = halves[2 * step + other][...]
+    batch, width = phi_ref.shape
+    scale = 4.0 / math.sqrt(width)
+    scores = scale * dot(phi_ref[...], psi_ref[...], ((1,), (1,)))
+    top = jnp.max(scores, axis=1, keepdims=True)
+    raised = jnp.exp(scores - top)
+    share = raised * (1.0 / jnp.sum(raised, axis=1, keepdims=True))
+    row_ids = lax.broadcasted_iota(jnp.int32, (batch, batch), 0)
+    col_ids = lax.broadcasted_iota(jnp.int32, (batch, batch), 1)
+    weights = (share - (row_ids == col_ids).astype(F32)).astype(BF16)
+    columns = grad_ref.shape[1] // shards
+    mine = pl.ds(pl.multiple_of(here * columns, columns), columns)
+    sides = (
+        (dot(weights, psi_ref[...]), state_x, state_act, state_slope, state_second, outs[:2]),
+        (dot(weights, phi_ref[...], ((0,), (0,))), goal_x, goal_act, goal_slope, goal_second, outs[2:]),
+    )
+    for grad, pieces, act_ref, slope_ref, second_ref, (first_out, second_out) in sides:
+        grad = (scale * grad).astype(BF16)
+        grad_ref[...] = grad
+        back = dot(grad, second_ref[...], ((1,), (1,)))
+        slope = (back * slope_ref[...]).astype(BF16)
+        for index in range(4):
+
+            @pl.when((group ^ index) == here)
+            def _(index=index):
+                column_ref[...] = pieces[index][...]
+
+        first_out[...] = dot(column_ref[...], slope, ((0,), (0,)))
+        second_out[...] = dot(act_ref[...], grad_ref[:, mine], ((0,), (0,)))
+
+
+def whole_batch(
+    replay, sa_row, goal_owner, goal_row, state_first, state_second, goal_first, goal_second
+):
+    shards = lax.axis_size("dp")
+    here = lax.axis_index("dp").astype(jnp.int32).reshape(1)
+    group = lax.axis_index("mp").astype(jnp.int32).reshape(1)
+    rows = sa_row.shape[0]
+    slots = 2 * rows // shards
+    width = replay.shape[1]
+    units, embed = state_second.shape
+    batch = shards * rows
+
+    def around(array):
+        turns = [[(i, (i + s) % shards) for i in range(shards)] for s in range(1, shards)]
+        return [array] + [lax.ppermute(array, "dp", turn) for turn in turns]
+
+    def swap(array, bit):
+        return lax.ppermute(array, "mp", [(i, i ^ bit) for i in range(4)])
+
+    want = jnp.concatenate([goal_owner.reshape(1, rows), goal_row.reshape(1, rows)], axis=0)
+    wants = around(want)
+    (state_mine,) = call(
+        pick_kernel, [((rows, width), BF16)], [sa_row.reshape(1, rows), replay], flops=2 * rows * replay.size
+    )
+    state_near = [state_mine] + [swap(state_mine, bit) for bit in (1, 2, 3)]
+    firsts = [goal_first, swap(goal_first, 1), swap(goal_first, 2)]
+    seconds = [goal_second, swap(goal_second, 1), swap(goal_second, 2)]
+    firsts.append(swap(firsts[2], 1))
+    seconds.append(swap(seconds[2], 1))
+    (found,) = call(
+        functools.partial(found_kernel, shards, slots),
+        [((shards * slots, width), BF16)],
+        [here, *wants, replay],
+        scalars=1,
+        scratch=[pltpu.VMEM((8, rows), F32)],
+        flops=2 * shards * slots * replay.size,
+    )
+    founds = around(found)
+    (places,) = call(
+        functools.partial(place_kernel, shards, slots),
+        [((rows, 8), F32)],
+        [here, *wants],
+        scalars=1,
+        scratch=[pltpu.VMEM((8, rows), F32)],
+    )
+    keep, send = call(
+        part_kernel,
+        [((rows // 2, embed), F32), ((rows // 2, embed), F32)],
+        [group, *state_near, state_first, state_second],
+        scalars=1,
+        scratch=[pltpu.VMEM((rows, embed), F32)],
+        flops=4 * rows * state_first.size,
+    )
+    chip = keep + swap(send, 1)
+    phi_half = (chip + swap(chip, 2)).astype(BF16)
+    phi_halves = []
+    for piece in around(phi_half):
+        phi_halves += [piece, swap(piece, 1)]
+    state_all = jnp.concatenate(around(state_mine), axis=0)
+    state_x = [state_all, swap(state_all, 1), swap(state_all, 2)]
+    state_x.append(swap(state_x[2], 1))
+    state_act, state_slope = call(
+        act_kernel,
+        [((batch, units), BF16), ((batch, units), F32)],
+        [group, *state_x, state_first],
+        scalars=1,
+        flops=2 * batch * state_first.size,
+    )
+    (goal_all,) = call(
+        functools.partial(select_kernel, shards),
+        [((batch, width), BF16)],
+        [places, *founds],
+        flops=2 * batch * shards * found.size,
+    )
+    goal_x = [goal_all, swap(goal_all, 1), swap(goal_all, 2)]
+    goal_x.append(swap(goal_x[2], 1))
+    psi, goal_act, goal_slope = call(
+        embed_kernel,
+        [((batch, embed), BF16), ((batch, units), BF16), ((batch, units), F32)],
+        [group, *goal_x, *firsts, *seconds],
+        scalars=1,
+        scratch=[pltpu.VMEM((batch, embed), F32)],
+        flops=16 * batch * goal_first.size,
+    )
+    latents = 4 * width // shards
+    outs = [((latents, units), F32), ((units, embed // shards), F32)]
+    return tuple(
+        call(
+            functools.partial(grads_kernel, shards),
+            outs + outs,
+            [group, here, *phi_halves, psi, *state_x, *goal_x]
+            + [state_act, state_slope, goal_act, goal_slope, state_second, goal_second],
+            scalars=2,
+            scratch=[
+                pltpu.VMEM((batch, embed), BF16),
+                pltpu.VMEM((batch, width), BF16),
+                pltpu.VMEM((batch, embed), BF16),
+            ],
+            flops=6 * batch * batch * embed + 6 * batch * state_first.size,
+        )
+    )
+
+
+def body(*args):
+    shards, models = lax.axis_size("dp"), lax.axis_size("mp")
+    rows = args[1].shape[0]
+    if models == 4 and shards == 4 and shards * rows <= 1024:
+        return whole_batch(*args)
+    return split_batch(*args)
+
+
 def solution(mesh):
     in_specs = (
         P(("groups", "dp"), "mp"),

time: 260 us -> 125 us (0.48)
  blocking collectives: 70 us -> 0 us
  waiting for transfers between devices: 131 us -> 67.6 us
  Pallas kernels: 0 us -> 19.3 us
  starting transfers between devices: 11.6 us -> 28.5 us
  between operations: 15.9 us -> 0.82 us
  other arithmetic: 13.5 us -> 0.76 us
  matrix products: 11.1 us -> 0 us
    reduce_scatter x5 -> x0, waiting for transfers between devices: 94 us -> none  [the longest x1 26.3 us: body(): lax.psum_scatter(goal_two.astype(jnp.bfloat16), 'dp', scatter_dimension=1...]
    ppermute x0 -> x33, waiting for transfers between devices: none -> 67.6 us  [the longest x21 35.5 us: swap(): return lax.ppermute(array, 'mp', [(i, i ^ bit) for i in range(4)])]
    psum x2 -> x0, blocking collectives: 32.6 us -> none  [the longest x1 26.6 us: body(): state_total, goal_total = lax.psum((state_part, goal_part), 'mp')]
    all_gather x4 -> x0, blocking collectives: 31.7 us -> none  [the longest x1 13.8 us: body(): psi_cols = lax.all_gather(psi_mine, 'dp', axis=0, tiled=True)]
    psum x1 -> x0, waiting for transfers between devices: 30.1 us -> none  [body(): phi_grad = lax.psum(row_part.astype(jnp.bfloat16), 'mp')]
    ppermute x0 -> x33, starting transfers between devices: none -> 28.5 us  [the longest x12 16.1 us: around(): return [array] + [lax.ppermute(array, 'dp', turn) for turn in turns]]
    pallas_call x0 -> x8, Pallas kernels: none -> 19.3 us  [call(): pl.pallas_call(kernel, out_shape=[jax.ShapeDtypeStruct(s, d) for s, d in...]
    all_to_all x2 -> x0, starting transfers between devices: 11.4 us -> none  [the longest x1 6.32 us: body(): lax.all_to_all(requests, 'dp', split_axis=0, concat_axis=0, tiled=True)]
  transfers between devices with their start and end apart: 8 -> 33, of which waited for: 6 -> 13; matrix products, arithmetic and copies ran while one was open for 7% -> 1% of each run, Pallas kernels for 0% -> 9%
where the time goes in v1:
time: 125 us
  waiting for transfers between devices  67.6 us (54%)
  starting transfers between devices  28.5 us (23%)
  Pallas kernels  19.3 us (15%)
  local copies, waits for them, and re-layouts  7.74 us (6%)
    ppermute x21, waiting for transfers between devices, swap(): return lax.ppermute(array, 'mp', [(i, i ^ bit) for i in range(4)])  35.5 us
    ppermute x12, waiting for transfers between devices, around(): return [array] + [lax.ppermute(array, 'dp', turn) for turn in turns]  32.1 us
    pallas_call x8, Pallas kernels, call(): pl.pallas_call(kernel, out_shape=[jax.ShapeDtypeStruct(s, d) for s, d in...  19.3 us
    ppermute x12, starting transfers between devices, around(): return [array] + [lax.ppermute(array, 'dp', turn) for turn in turns]  16.1 us
    ppermute x21, starting transfers between devices, swap(): return lax.ppermute(array, 'mp', [(i, i ^ bit) for i in range(4)])  12.4 us
    unnamed x24, local copies, waits for them, and re-layouts  7.74 us
  transfers between devices with their start and end apart: 33, of which 13 were waited for; matrix products, arithmetic and copies ran while one was open for 1% of the time, Pallas kernels for 9%

profile of v1, /device:TPU:0, one launch (start us, length us, event | category | flops | bytes accessed | tf_op | source)
XLA Modules:
  0.0 124.7 jit_solution(15424294582474649956)
XLA Ops:
  0.6 3.0 %collective-permute-start.22 = (bf16[1024,512]{1,0:T(8,128)(2,1)}, bf16[1024,512]{1,0:T(8,128)(2,1)}, u32[]{:S(2)}, u32[]{:S(2)}) collective-permute-start(bf16[1024,512]{1,0:T(8,128)(2,1)} %refs_4_.6), channel_id=1, source_target_pairs={{0,2},{1,3},{2,0},{3,1},{4,6},{5,7},{6,4},{7,5},{8,10},{9,11},{10,... | collective-permute-start | bytes 3145736 | tf_op jit(solution)/shard_map/ppermute | solution.py:313
  3.6 0.1 collective-permute-start.25
  3.7 1.0 copy-done.1
  4.8 0.7 copy-done.4
  5.4 0.3 shard_map.111.refs_0_
  5.8 2.1 %collective-permute-start.27 = (bf16[128,256]{1,0:T(8,128)(2,1)S(1)}, bf16[128,256]{1,0:T(8,128)(2,1)S(1)}, u32[]{:S(2)}, u32[]{:S(2)}) collective-permute-start(bf16[128,256]{1,0:T(8,128)(2,1)S(1)} %shard_map.111.refs_0_), channel_id=1, source_target_pairs={{0,4},{4,8},{8,12},{12,0},{1,5},{5,9},{9,13},{13,1},{2,6},{6,10},{... | collective-permute-start | bytes 196616 | tf_op jit(solution)/shard_map/ppermute | solution.py:310
  7.9 2.6 %collective-permute-start.28 = (bf16[128,256]{1,0:T(8,128)(2,1)S(1)}, bf16[128,256]{1,0:T(8,128)(2,1)S(1)}, u32[]{:S(2)}, u32[]{:S(2)}) collective-permute-start(bf16[128,256]{1,0:T(8,128)(2,1)S(1)} %shard_map.111.refs_0_), channel_id=1, source_target_pairs={{0,8},{4,12},{8,0},{12,4},{1,9},{5,13},{9,1},{13,5},{2,10},{6,14},... | collective-permute-start | bytes 196616 | tf_op jit(solution)/shard_map/ppermute | solution.py:310
  10.4 0.7 pad_add_fusion.refs_0_
  11.1 0.1 collective-permute-start.12
  11.2 5.3 %collective-permute-done.12.refs_1_ = s32[2,128]{1,0:T(2,128)S(1)} collective-permute-done((s32[2,128]{1,0:T(2,128)S(1)}, s32[2,128]{1,0:T(2,128)S(1)}, u32[]{:S(2)}, u32[]{:S(2)}) %collective-permute-start.12) | collective-permute-done | bytes 1056 | tf_op jit(solution)/shard_map/ppermute | solution.py:310
  16.5 4.5 %collective-permute-done.13.refs_2_ = s32[2,128]{1,0:T(2,128)S(1)} collective-permute-done((s32[2,128]{1,0:T(2,128)S(1)}, s32[2,128]{1,0:T(2,128)S(1)}, u32[]{:S(2)}, u32[]{:S(2)}) %collective-permute-start.13) | collective-permute-done | bytes 1056 | tf_op jit(solution)/shard_map/ppermute | solution.py:310
  21.0 3.6 %collective-permute-done.14.refs_3_ = s32[2,128]{1,0:T(2,128)S(1)} collective-permute-done((s32[2,128]{1,0:T(2,128)S(1)}, s32[2,128]{1,0:T(2,128)S(1)}, u32[]{:S(2)}, u32[]{:S(2)}) %collective-permute-start.14) | collective-permute-done | bytes 1056 | tf_op jit(solution)/shard_map/ppermute | solution.py:310
  24.5 1.8 %collective-permute-start.29 = (bf16[128,256]{1,0:T(8,128)(2,1)S(1)}, bf16[128,256]{1,0:T(8,128)(2,1)S(1)}, u32[]{:S(2)}, u32[]{:S(2)}) collective-permute-start(bf16[128,256]{1,0:T(8,128)(2,1)S(1)} %shard_map.111.refs_0_), channel_id=1, source_target_pairs={{0,12},{4,0},{8,4},{12,8},{1,13},{5,1},{9,5},{13,9},{2,14},{6,2},{... | collective-permute-start | bytes 196616 | tf_op jit(solution)/shard_map/ppermute | solution.py:310
  26.3 0.0 collective-permute-start
  26.3 0.0 collective-permute-done.28
  26.4 1.6 %collective-permute-start.1 = (bf16[128,256]{1,0:T(8,128)(2,1)S(1)}, bf16[128,256]{1,0:T(8,128)(2,1)S(1)}, u32[]{:S(2)}, u32[]{:S(2)}) collective-permute-start(bf16[128,256]{1,0:T(8,128)(2,1)S(1)} %shard_map.111.refs_0_), channel_id=1, source_target_pairs={{0,2},{1,3},{2,0},{3,1},{4,6},{5,7},{6,4},{7,5},{8,10},{9,11},{10,... | collective-permute-start | bytes 196616 | tf_op jit(solution)/shard_map/ppermute | solution.py:313
  27.9 0.9 collective-permute-done.29
  28.8 0.0 collective-permute-start.2
  28.8 1.0 copy-done.2
  29.8 0.7 shard_map.114.refs_0_
  30.6 0.0 collective-permute-done.refs_1_
  30.6 0.1 collective-permute-start.15
  30.6 21.0 %collective-permute-done.1.refs_2_ = bf16[128,256]{1,0:T(8,128)(2,1)S(1)} collective-permute-done((bf16[128,256]{1,0:T(8,128)(2,1)S(1)}, bf16[128,256]{1,0:T(8,128)(2,1)S(1)}, u32[]{:S(2)}, u32[]{:S(2)}) %collective-permute-start.1) | collective-permute-done | bytes 65568 | tf_op jit(solution)/shard_map/ppermute | solution.py:313
  51.6 2.8 %collective-permute-start.16 = (bf16[256,256]{1,0:T(8,128)(2,1)S(1)}, bf16[256,256]{1,0:T(8,128)(2,1)S(1)}, u32[]{:S(2)}, u32[]{:S(2)}) collective-permute-start(bf16[256,256]{1,0:T(8,128)(2,1)S(1)} %shard_map.114.refs_0_), channel_id=1, source_target_pairs={{0,8},{4,12},{8,0},{12,4},{1,9},{5,13},{9,1},{13,5},{2,10},{6,14},... | collective-permute-start | bytes 393224 | tf_op jit(solution)/shard_map/ppermute | solution.py:310
  54.4 0.0 collective-permute-done.2.refs_3_
  54.4 1.3 %collective-permute-start.17 = (bf16[256,256]{1,0:T(8,128)(2,1)S(1)}, bf16[256,256]{1,0:T(8,128)(2,1)S(1)}, u32[]{:S(2)}, u32[]{:S(2)}) collective-permute-start(bf16[256,256]{1,0:T(8,128)(2,1)S(1)} %shard_map.114.refs_0_), channel_id=1, source_target_pairs={{0,12},{4,0},{8,4},{12,8},{1,13},{5,1},{9,5},{13,9},{2,14},{6,2},{... | collective-permute-start | bytes 393224 | tf_op jit(solution)/shard_map/ppermute | solution.py:310
  55.8 0.0 collective-permute-done.15.refs_1_
  55.8 1.6 %collective-permute-start.31 = (bf16[512,256]{1,0:T(8,128)(2,1)S(1)}, bf16[512,256]{1,0:T(8,128)(2,1)S(1)}, u32[]{:S(2)}, u32[]{:S(2)}) collective-permute-start(bf16[512,256]{1,0:T(8,128)(2,1)S(1)} %pad_maximum_fusion.refs_0_.refs_9_), channel_id=1, source_target_pairs={{0,2},{1,3},{2,0},{3,1},{4,6},{5,7},{6,4},{7,5},{8,10},{9,11},{10,... | collective-permute-start | bytes 786440 | tf_op jit(solution)/shard_map/ppermute | solution.py:313
  57.4 3.1 %collective-permute-done.16.refs_2_ = bf16[256,256]{1,0:T(8,128)(2,1)S(1)} collective-permute-done((bf16[256,256]{1,0:T(8,128)(2,1)S(1)}, bf16[256,256]{1,0:T(8,128)(2,1)S(1)}, u32[]{:S(2)}, u32[]{:S(2)}) %collective-permute-start.16) | collective-permute-done | bytes 131104 | tf_op jit(solution)/shard_map/ppermute | solution.py:310
  60.5 0.0 collective-permute-start.30
  60.5 1.2 copy-done.3
  61.7 0.6 shard_map.112
  62.4 0.0 copy-start.5
  62.4 0.0 collective-permute-done.17.refs_3_
  62.4 0.6 collective-permute-start.3
  63.0 0.3 shard_map.113.place_ref
  63.2 0.5 shard_map.115.refs_0_.refs_13_
  63.8 0.2 collective-permute-done.31.refs_2_.refs_11_
  64.0 1.5 %collective-permute-start.19 = (bf16[512,256]{1,0:T(8,128)(2,1)S(1)}, bf16[512,256]{1,0:T(8,128)(2,1)S(1)}, u32[]{:S(2)}, u32[]{:S(2)}) collective-permute-start(bf16[512,256]{1,0:T(8,128)(2,1)S(1)} %shard_map.115.refs_0_.refs_13_), channel_id=1, source_target_pairs={{0,2},{1,3},{2,0},{3,1},{4,6},{5,7},{6,4},{7,5},{8,10},{9,11},{10,... | collective-permute-start | bytes 786440 | tf_op jit(solution)/shard_map/ppermute | solution.py:313
  65.5 0.0 collective-permute-done.30.refs_1_.refs_10_
  65.5 0.5 collective-permute-start.32
  66.0 6.1 %collective-permute-done.19.refs_2_.refs_15_ = bf16[512,256]{1,0:T(8,128)(2,1)S(1)} collective-permute-done((bf16[512,256]{1,0:T(8,128)(2,1)S(1)}, bf16[512,256]{1,0:T(8,128)(2,1)S(1)}, u32[]{:S(2)}, u32[]{:S(2)}) %collective-permute-start.19) | collective-permute-done | bytes 262176 | tf_op jit(solution)/shard_map/ppermute | solution.py:313
  72.1 0.5 collective-permute-start.24
  72.6 0.1 collective-permute-start.23
  72.7 0.4 collective-permute-start.26
  73.2 1.6 %collective-permute-start.4 = (f32[64,1024]{1,0:T(8,128)S(1)}, f32[64,1024]{1,0:T(8,128)S(1)}, u32[]{:S(2)}, u32[]{:S(2)}) collective-permute-start(f32[64,1024]{1,0:T(8,128)S(1)} %add.6), channel_id=1, source_target_pairs={{0,2},{1,3},{2,0},{3,1},{4,6},{5,7},{6,4},{7,5},{8,10},{9,11},{10,... | collective-permute-start | bytes 786440 | tf_op jit(solution)/shard_map/ppermute | solution.py:313
  74.8 6.7 %collective-permute-done.4 = f32[64,1024]{1,0:T(8,128)S(1)} collective-permute-done((f32[64,1024]{1,0:T(8,128)S(1)}, f32[64,1024]{1,0:T(8,128)S(1)}, u32[]{:S(2)}, u32[]{:S(2)}) %collective-permute-start.4) | collective-permute-done | bytes 262176 | tf_op jit(solution)/shard_map/ppermute | solution.py:313
  81.6 1.5 %collective-permute-done.20.refs_3_.refs_16_ = bf16[512,256]{1,0:T(8,128)(2,1)S(1)} collective-permute-done((bf16[512,256]{1,0:T(8,128)(2,1)S(1)}, bf16[512,256]{1,0:T(8,128)(2,1)S(1)}, u32[]{:S(2)}, u32[]{:S(2)}) %collective-permute-start.20) | collective-permute-done | bytes 262176 | tf_op jit(solution)/shard_map/ppermute | solution.py:313
  83.1 5.1 %collective-permute-start.10 = (bf16[64,1024]{1,0:T(8,128)(2,1)S(1)}, bf16[64,1024]{1,0:T(8,128)(2,1)S(1)}, u32[]{:S(2)}, u32[]{:S(2)}) collective-permute-start(bf16[64,1024]{1,0:T(8,128)(2,1)S(1)} %add_convert_fusion.refs_0_), channel_id=1, source_target_pairs={{0,12},{4,0},{8,4},{12,8},{1,13},{5,1},{9,5},{13,9},{2,14},{6,2},{... | collective-permute-start | bytes 393224 | tf_op jit(solution)/shard_map/ppermute | solution.py:310
  88.2 3.3 %collective-permute-done.10.refs_6_ = bf16[64,1024]{1,0:T(8,128)(2,1)S(1)} collective-permute-done((bf16[64,1024]{1,0:T(8,128)(2,1)S(1)}, bf16[64,1024]{1,0:T(8,128)(2,1)S(1)}, u32[]{:S(2)}, u32[]{:S(2)}) %collective-permute-start.10) | collective-permute-done | bytes 131104 | tf_op jit(solution)/shard_map/ppermute | solution.py:310
  91.5 7.2 %collective-permute-done.6.refs_2_ = bf16[64,1024]{1,0:T(8,128)(2,1)S(1)} collective-permute-done((bf16[64,1024]{1,0:T(8,128)(2,1)S(1)}, bf16[64,1024]{1,0:T(8,128)(2,1)S(1)}, u32[]{:S(2)}, u32[]{:S(2)}) %collective-permute-start.6) | collective-permute-done | bytes 131104 | tf_op jit(solution)/shard_map/ppermute | solution.py:310
  98.7 0.1 collective-permute-start.8
  98.8 1.0 shard_map.117
  99.8 1.0 copy-done.6
  100.8 4.3 %collective-permute-done.8.refs_4_ = bf16[64,1024]{1,0:T(8,128)(2,1)S(1)} collective-permute-done((bf16[64,1024]{1,0:T(8,128)(2,1)S(1)}, bf16[64,1024]{1,0:T(8,128)(2,1)S(1)}, u32[]{:S(2)}, u32[]{:S(2)}) %collective-permute-start.8) | collective-permute-done | bytes 131104 | tf_op jit(solution)/shard_map/ppermute | solution.py:310
  105.1 0.5 collective-permute-start.11
  105.6 0.1 collective-permute-start.7
  105.7 0.4 collective-permute-start.9
  106.2 0.5 copy-done.9
  106.6 0.3 copy-done.10
  107.0 1.0 copy-done.11
  107.9 8.0 %shard_map.116 = (bf16[512,1024]{1,0:T(8,128)(2,1)S(1)}, bf16[512,512]{1,0:T(8,128)(2,1)S(1)}, f32[512,512]{1,0:T(8,128)S(1)}) custom-call(s32[1]{0:T(128)} %bitcast.group_ref, bf16[512,256]{1,0:T(8,128)(2,1)S(1)} %shard_map.115.refs_0_.refs_13_, bf16[512,256]{1,0:T(8,128)(2,1)S(1)} %collective-permute-done.18.refs_1_.refs_14_, ...), custom_call_target="tpu_custom_call" | custom-call | flops 4294967296 | bytes 12058628 | tf_op jit(solution)/shard_map/pallas_call | solution.py:118
  116.0 1.0 copy-done.7
  117.0 7.7 %shard_map.118 = (f32[256,512]{1,0:T(8,128)}, f32[512,256]{1,0:T(8,128)}, f32[256,512]{1,0:T(8,128)}, f32[512,256]{1,0:T(8,128)}) custom-call(s32[1]{0:T(128)} %bitcast.group_ref, s32[1]{0:T(128)} %bitcast.1.here_ref, bf16[64,1024]{1,0:T(8,128)(2,1)S(1)} %add_convert_fusion.refs_0_, bf16[64,1024]{1,0:T(8,128)(2,1)S(1)} %collective-permute-done.5.refs_1_, ...), custom_call_target="tpu_custom_call" | custom-call | flops 3221225472 | bytes 11534344 | tf_op jit(solution)/shard_map/pallas_call | solution.py:118
  (38 shorter events, 0.2 us)
Async XLA Ops:
  0.6 59.9 %copy-start = (bf16[1024,512]{1,0:T(8,128)(2,1)S(1)}, bf16[1024,512]{1,0:T(8,128)(2,1)}, u32[]{:S(2)}) copy-start(bf16[1024,512]{1,0:T(8,128)(2,1)} %refs_4_.7) | copy-start | bytes 3145732
  0.6 72.0 %collective-permute-start.22 = (bf16[1024,512]{1,0:T(8,128)(2,1)}, bf16[1024,512]{1,0:T(8,128)(2,1)}, u32[]{:S(2)}, u32[]{:S(2)}) collective-permute-start(bf16[1024,512]{1,0:T(8,128)(2,1)} %refs_4_.6), channel_id=1, source_target_pairs={{0,2},{1,3},{2,0},{3,1},{4,6},{5,7},{6,4},{7,5},{8,10},{9,11},{10,... | collective-permute-start | bytes 3145736 | tf_op jit(solution)/shard_map/ppermute | solution.py:313
  3.6 69.0 %collective-permute-start.25 = (bf16[512,1024]{1,0:T(8,128)(2,1)}, bf16[512,1024]{1,0:T(8,128)(2,1)}, u32[]{:S(2)}, u32[]{:S(2)}) collective-permute-start(bf16[512,1024]{1,0:T(8,128)(2,1)} %refs_22_.1), channel_id=1, source_target_pairs={{0,2},{1,3},{2,0},{3,1},{4,6},{5,7},{6,4},{7,5},{8,10},{9,11},{10,... | collective-permute-start | bytes 3145736 | tf_op jit(solution)/shard_map/ppermute | solution.py:313
  3.7 1.0 copy-start.1
  4.8 0.7 copy-start.4
  5.8 20.6 %collective-permute-start.27 = (bf16[128,256]{1,0:T(8,128)(2,1)S(1)}, bf16[128,256]{1,0:T(8,128)(2,1)S(1)}, u32[]{:S(2)}, u32[]{:S(2)}) collective-permute-start(bf16[128,256]{1,0:T(8,128)(2,1)S(1)} %shard_map.111.refs_0_), channel_id=1, source_target_pairs={{0,4},{4,8},{8,12},{12,0},{1,5},{5,9},{9,13},{13,1},{2,6},{6,10},{... | collective-permute-start | bytes 196616 | tf_op jit(solution)/shard_map/ppermute | solution.py:310
  7.9 18.5 %collective-permute-start.28 = (bf16[128,256]{1,0:T(8,128)(2,1)S(1)}, bf16[128,256]{1,0:T(8,128)(2,1)S(1)}, u32[]{:S(2)}, u32[]{:S(2)}) collective-permute-start(bf16[128,256]{1,0:T(8,128)(2,1)S(1)} %shard_map.111.refs_0_), channel_id=1, source_target_pairs={{0,8},{4,12},{8,0},{12,4},{1,9},{5,13},{9,1},{13,5},{2,10},{6,14},... | collective-permute-start | bytes 196616 | tf_op jit(solution)/shard_map/ppermute | solution.py:310
  11.1 5.4 %collective-permute-start.12 = (s32[2,128]{1,0:T(2,128)S(1)}, s32[2,128]{1,0:T(2,128)S(1)}, u32[]{:S(2)}, u32[]{:S(2)}) collective-permute-start(s32[2,128]{1,0:T(2,128)S(1)} %pad_add_fusion.refs_0_), channel_id=1, source_target_pairs={{0,4},{4,8},{8,12},{12,0},{1,5},{5,9},{9,13},{13,1},{2,6},{6,10},{... | collective-permute-start | bytes 3080 | tf_op jit(solution)/shard_map/ppermute | solution.py:310
  16.5 4.5 %collective-permute-start.13 = (s32[2,128]{1,0:T(2,128)S(1)}, s32[2,128]{1,0:T(2,128)S(1)}, u32[]{:S(2)}, u32[]{:S(2)}) collective-permute-start(s32[2,128]{1,0:T(2,128)S(1)} %pad_add_fusion.refs_0_), channel_id=1, source_target_pairs={{0,8},{4,12},{8,0},{12,4},{1,9},{5,13},{9,1},{13,5},{2,10},{6,14},... | collective-permute-start | bytes 3080 | tf_op jit(solution)/shard_map/ppermute | solution.py:310
  21.0 3.6 %collective-permute-start.14 = (s32[2,128]{1,0:T(2,128)S(1)}, s32[2,128]{1,0:T(2,128)S(1)}, u32[]{:S(2)}, u32[]{:S(2)}) collective-permute-start(s32[2,128]{1,0:T(2,128)S(1)} %pad_add_fusion.refs_0_), channel_id=1, source_target_pairs={{0,12},{4,0},{8,4},{12,8},{1,13},{5,1},{9,5},{13,9},{2,14},{6,2},{... | collective-permute-start | bytes 3080 | tf_op jit(solution)/shard_map/ppermute | solution.py:310
  24.5 4.3 %collective-permute-start.29 = (bf16[128,256]{1,0:T(8,128)(2,1)S(1)}, bf16[128,256]{1,0:T(8,128)(2,1)S(1)}, u32[]{:S(2)}, u32[]{:S(2)}) collective-permute-start(bf16[128,256]{1,0:T(8,128)(2,1)S(1)} %shard_map.111.refs_0_), channel_id=1, source_target_pairs={{0,12},{4,0},{8,4},{12,8},{1,13},{5,1},{9,5},{13,9},{2,14},{6,2},{... | collective-permute-start | bytes 196616 | tf_op jit(solution)/shard_map/ppermute | solution.py:310
  26.3 4.2 %collective-permute-start = (bf16[128,256]{1,0:T(8,128)(2,1)S(1)}, bf16[128,256]{1,0:T(8,128)(2,1)S(1)}, u32[]{:S(2)}, u32[]{:S(2)}) collective-permute-start(bf16[128,256]{1,0:T(8,128)(2,1)S(1)} %shard_map.111.refs_0_), channel_id=1, source_target_pairs={{0,1},{1,0},{2,3},{3,2},{4,5},{5,4},{6,7},{7,6},{8,9},{9,8},{10,11... | collective-permute-start | bytes 196616 | tf_op jit(solution)/shard_map/ppermute | solution.py:313
  26.4 25.2 %collective-permute-start.1 = (bf16[128,256]{1,0:T(8,128)(2,1)S(1)}, bf16[128,256]{1,0:T(8,128)(2,1)S(1)}, u32[]{:S(2)}, u32[]{:S(2)}) collective-permute-start(bf16[128,256]{1,0:T(8,128)(2,1)S(1)} %shard_map.111.refs_0_), channel_id=1, source_target_pairs={{0,2},{1,3},{2,0},{3,1},{4,6},{5,7},{6,4},{7,5},{8,10},{9,11},{10,... | collective-permute-start | bytes 196616 | tf_op jit(solution)/shard_map/ppermute | solution.py:313
  28.8 25.6 %collective-permute-start.2 = (bf16[128,256]{1,0:T(8,128)(2,1)S(1)}, bf16[128,256]{1,0:T(8,128)(2,1)S(1)}, u32[]{:S(2)}, u32[]{:S(2)}) collective-permute-start(bf16[128,256]{1,0:T(8,128)(2,1)S(1)} %shard_map.111.refs_0_), channel_id=1, source_target_pairs={{0,3},{1,2},{2,1},{3,0},{4,7},{5,6},{6,5},{7,4},{8,11},{9,10},{10,... | collective-permute-start | bytes 196616 | tf_op jit(solution)/shard_map/ppermute | solution.py:313
  28.8 1.0 copy-start.2
  30.6 25.2 %collective-permute-start.15 = (bf16[256,256]{1,0:T(8,128)(2,1)S(1)}, bf16[256,256]{1,0:T(8,128)(2,1)S(1)}, u32[]{:S(2)}, u32[]{:S(2)}) collective-permute-start(bf16[256,256]{1,0:T(8,128)(2,1)S(1)} %shard_map.114.refs_0_), channel_id=1, source_target_pairs={{0,4},{4,8},{8,12},{12,0},{1,5},{5,9},{9,13},{13,1},{2,6},{6,10},{... | collective-permute-start | bytes 393224 | tf_op jit(solution)/shard_map/ppermute | solution.py:310
  51.6 8.9 %collective-permute-start.16 = (bf16[256,256]{1,0:T(8,128)(2,1)S(1)}, bf16[256,256]{1,0:T(8,128)(2,1)S(1)}, u32[]{:S(2)}, u32[]{:S(2)}) collective-permute-start(bf16[256,256]{1,0:T(8,128)(2,1)S(1)} %shard_map.114.refs_0_), channel_id=1, source_target_pairs={{0,8},{4,12},{8,0},{12,4},{1,9},{5,13},{9,1},{13,5},{2,10},{6,14},... | collective-permute-start | bytes 393224 | tf_op jit(solution)/shard_map/ppermute | solution.py:310
  54.4 8.0 %collective-permute-start.17 = (bf16[256,256]{1,0:T(8,128)(2,1)S(1)}, bf16[256,256]{1,0:T(8,128)(2,1)S(1)}, u32[]{:S(2)}, u32[]{:S(2)}) collective-permute-start(bf16[256,256]{1,0:T(8,128)(2,1)S(1)} %shard_map.114.refs_0_), channel_id=1, source_target_pairs={{0,12},{4,0},{8,4},{12,8},{1,13},{5,1},{9,5},{13,9},{2,14},{6,2},{... | collective-permute-start | bytes 393224 | tf_op jit(solution)/shard_map/ppermute | solution.py:310
  55.8 8.2 %collective-permute-start.31 = (bf16[512,256]{1,0:T(8,128)(2,1)S(1)}, bf16[512,256]{1,0:T(8,128)(2,1)S(1)}, u32[]{:S(2)}, u32[]{:S(2)}) collective-permute-start(bf16[512,256]{1,0:T(8,128)(2,1)S(1)} %pad_maximum_fusion.refs_0_.refs_9_), channel_id=1, source_target_pairs={{0,2},{1,3},{2,0},{3,1},{4,6},{5,7},{6,4},{7,5},{8,10},{9,11},{10,... | collective-permute-start | bytes 786440 | tf_op jit(solution)/shard_map/ppermute | solution.py:313
  60.5 5.0 %collective-permute-start.30 = (bf16[512,256]{1,0:T(8,128)(2,1)S(1)}, bf16[512,256]{1,0:T(8,128)(2,1)S(1)}, u32[]{:S(2)}, u32[]{:S(2)}) collective-permute-start(bf16[512,256]{1,0:T(8,128)(2,1)S(1)} %pad_maximum_fusion.refs_0_.refs_9_), channel_id=1, source_target_pairs={{0,1},{1,0},{2,3},{3,2},{4,5},{5,4},{6,7},{7,6},{8,9},{9,8},{10,11... | collective-permute-start | bytes 786440 | tf_op jit(solution)/shard_map/ppermute | solution.py:313
  60.5 1.2 copy-start.3
  61.7 10.4 %copy-start.8 = (bf16[512,1024]{1,0:T(8,128)(2,1)S(1)}, bf16[512,1024]{1,0:T(8,128)(2,1)}, u32[]{:S(2)}) copy-start(bf16[512,1024]{1,0:T(8,128)(2,1)} %refs_22_.1) | copy-start | bytes 3145732
  62.4 9.7 %copy-start.5 = (bf16[1024,512]{1,0:T(8,128)(2,1)S(1)}, bf16[1024,512]{1,0:T(8,128)(2,1)}, u32[]{:S(2)}) copy-start(bf16[1024,512]{1,0:T(8,128)(2,1)} %refs_4_.6) | copy-start | bytes 3145732
  62.4 3.1 %collective-permute-start.3 = (f32[64,1024]{1,0:T(8,128)S(1)}, f32[64,1024]{1,0:T(8,128)S(1)}, u32[]{:S(2)}, u32[]{:S(2)}) collective-permute-start(f32[64,1024]{1,0:T(8,128)S(1)} %get-tuple-element.12), channel_id=1, source_target_pairs={{0,1},{1,0},{2,3},{3,2},{4,5},{5,4},{6,7},{7,6},{8,9},{9,8},{10,11... | collective-permute-start | bytes 786440 | tf_op jit(solution)/shard_map/ppermute | solution.py:313
  64.0 8.1 %collective-permute-start.19 = (bf16[512,256]{1,0:T(8,128)(2,1)S(1)}, bf16[512,256]{1,0:T(8,128)(2,1)S(1)}, u32[]{:S(2)}, u32[]{:S(2)}) collective-permute-start(bf16[512,256]{1,0:T(8,128)(2,1)S(1)} %shard_map.115.refs_0_.refs_13_), channel_id=1, source_target_pairs={{0,2},{1,3},{2,0},{3,1},{4,6},{5,7},{6,4},{7,5},{8,10},{9,11},{10,... | collective-permute-start | bytes 786440 | tf_op jit(solution)/shard_map/ppermute | solution.py:313
  65.5 6.6 %collective-permute-start.18 = (bf16[512,256]{1,0:T(8,128)(2,1)S(1)}, bf16[512,256]{1,0:T(8,128)(2,1)S(1)}, u32[]{:S(2)}, u32[]{:S(2)}) collective-permute-start(bf16[512,256]{1,0:T(8,128)(2,1)S(1)} %shard_map.115.refs_0_.refs_13_), channel_id=1, source_target_pairs={{0,1},{1,0},{2,3},{3,2},{4,5},{5,4},{6,7},{7,6},{8,9},{9,8},{10,11... | collective-permute-start | bytes 786440 | tf_op jit(solution)/shard_map/ppermute | solution.py:313
  65.5 7.7 %collective-permute-start.32 = (bf16[512,256]{1,0:T(8,128)(2,1)S(1)}, bf16[512,256]{1,0:T(8,128)(2,1)S(1)}, u32[]{:S(2)}, u32[]{:S(2)}) collective-permute-start(bf16[512,256]{1,0:T(8,128)(2,1)S(1)} %collective-permute-done.31.refs_2_.refs_11_), channel_id=1, source_target_pairs={{0,1},{1,0},{2,3},{3,2},{4,5},{5,4},{6,7},{7,6},{8,9},{9,8},{10,11... | collective-permute-start | bytes 786440 | tf_op jit(solution)/shard_map/ppermute | solution.py:313
  72.1 33.0 %collective-permute-start.21 = (bf16[1024,512]{1,0:T(8,128)(2,1)S(1)}, bf16[1024,512]{1,0:T(8,128)(2,1)S(1)}, u32[]{:S(2)}, u32[]{:S(2)}) collective-permute-start(bf16[1024,512]{1,0:T(8,128)(2,1)S(1)} %copy-done.5), channel_id=1, source_target_pairs={{0,1},{1,0},{2,3},{3,2},{4,5},{5,4},{6,7},{7,6},{8,9},{9,8},{10,11... | collective-permute-start | bytes 3145736 | tf_op jit(solution)/shard_map/ppermute | solution.py:313
  72.1 33.5 %collective-permute-start.24 = (bf16[512,1024]{1,0:T(8,128)(2,1)S(1)}, bf16[512,1024]{1,0:T(8,128)(2,1)S(1)}, u32[]{:S(2)}, u32[]{:S(2)}) collective-permute-start(bf16[512,1024]{1,0:T(8,128)(2,1)S(1)} %copy-done.8), channel_id=1, source_target_pairs={{0,1},{1,0},{2,3},{3,2},{4,5},{5,4},{6,7},{7,6},{8,9},{9,8},{10,11... | collective-permute-start | bytes 3145736 | tf_op jit(solution)/shard_map/ppermute | solution.py:313
  72.6 33.1 %collective-permute-start.23 = (bf16[1024,512]{1,0:T(8,128)(2,1)}, bf16[1024,512]{1,0:T(8,128)(2,1)S(1)}, u32[]{:S(2)}, u32[]{:S(2)}) collective-permute-start(bf16[1024,512]{1,0:T(8,128)(2,1)} %collective-permute-done.22.refs_6_), channel_id=1, source_target_pairs={{0,1},{1,0},{2,3},{3,2},{4,5},{5,4},{6,7},{7,6},{8,9},{9,8},{10,11... | collective-permute-start | bytes 3145736 | tf_op jit(solution)/shard_map/ppermute | solution.py:313
  72.7 33.5 %collective-permute-start.26 = (bf16[512,1024]{1,0:T(8,128)(2,1)}, bf16[512,1024]{1,0:T(8,128)(2,1)S(1)}, u32[]{:S(2)}, u32[]{:S(2)}) collective-permute-start(bf16[512,1024]{1,0:T(8,128)(2,1)} %collective-permute-done.25.refs_10_), channel_id=1, source_target_pairs={{0,1},{1,0},{2,3},{3,2},{4,5},{5,4},{6,7},{7,6},{8,9},{9,8},{10,11... | collective-permute-start | bytes 3145736 | tf_op jit(solution)/shard_map/ppermute | solution.py:313
  73.2 8.4 %collective-permute-start.4 = (f32[64,1024]{1,0:T(8,128)S(1)}, f32[64,1024]{1,0:T(8,128)S(1)}, u32[]{:S(2)}, u32[]{:S(2)}) collective-permute-start(f32[64,1024]{1,0:T(8,128)S(1)} %add.6), channel_id=1, source_target_pairs={{0,2},{1,3},{2,0},{3,1},{4,6},{5,7},{6,4},{7,5},{8,10},{9,11},{10,... | collective-permute-start | bytes 786440 | tf_op jit(solution)/shard_map/ppermute | solution.py:313
  81.5 1.5 %collective-permute-start.20 = (bf16[512,256]{1,0:T(8,128)(2,1)S(1)}, bf16[512,256]{1,0:T(8,128)(2,1)S(1)}, u32[]{:S(2)}, u32[]{:S(2)}) collective-permute-start(bf16[512,256]{1,0:T(8,128)(2,1)S(1)} %collective-permute-done.19.refs_2_.refs_15_), channel_id=1, source_target_pairs={{0,1},{1,0},{2,3},{3,2},{4,5},{5,4},{6,7},{7,6},{8,9},{9,8},{10,11... | collective-permute-start | bytes 786440 | tf_op jit(solution)/shard_map/ppermute | solution.py:313
  83.1 8.4 %collective-permute-start.10 = (bf16[64,1024]{1,0:T(8,128)(2,1)S(1)}, bf16[64,1024]{1,0:T(8,128)(2,1)S(1)}, u32[]{:S(2)}, u32[]{:S(2)}) collective-permute-start(bf16[64,1024]{1,0:T(8,128)(2,1)S(1)} %add_convert_fusion.refs_0_), channel_id=1, source_target_pairs={{0,12},{4,0},{8,4},{12,8},{1,13},{5,1},{9,5},{13,9},{2,14},{6,2},{... | collective-permute-start | bytes 393224 | tf_op jit(solution)/shard_map/ppermute | solution.py:310
  91.5 7.2 %collective-permute-start.6 = (bf16[64,1024]{1,0:T(8,128)(2,1)S(1)}, bf16[64,1024]{1,0:T(8,128)(2,1)S(1)}, u32[]{:S(2)}, u32[]{:S(2)}) collective-permute-start(bf16[64,1024]{1,0:T(8,128)(2,1)S(1)} %add_convert_fusion.refs_0_), channel_id=1, source_target_pairs={{0,4},{4,8},{8,12},{12,0},{1,5},{5,9},{9,13},{13,1},{2,6},{6,10},{... | collective-permute-start | bytes 393224 | tf_op jit(solution)/shard_map/ppermute | solution.py:310
  98.7 6.4 %collective-permute-start.8 = (bf16[64,1024]{1,0:T(8,128)(2,1)S(1)}, bf16[64,1024]{1,0:T(8,128)(2,1)S(1)}, u32[]{:S(2)}, u32[]{:S(2)}) collective-permute-start(bf16[64,1024]{1,0:T(8,128)(2,1)S(1)} %add_convert_fusion.refs_0_), channel_id=1, source_target_pairs={{0,8},{4,12},{8,0},{12,4},{1,9},{5,13},{9,1},{13,5},{2,10},{6,14},... | collective-permute-start | bytes 393224 | tf_op jit(solution)/shard_map/ppermute | solution.py:310
  99.8 1.0 copy-start.6
  105.1 11.9 %collective-permute-start.5 = (bf16[64,1024]{1,0:T(8,128)(2,1)S(1)}, bf16[64,1024]{1,0:T(8,128)(2,1)S(1)}, u32[]{:S(2)}, u32[]{:S(2)}) collective-permute-start(bf16[64,1024]{1,0:T(8,128)(2,1)S(1)} %add_convert_fusion.refs_0_), channel_id=1, source_target_pairs={{0,1},{1,0},{2,3},{3,2},{4,5},{5,4},{6,7},{7,6},{8,9},{9,8},{10,11... | collective-permute-start | bytes 393224 | tf_op jit(solution)/shard_map/ppermute | solution.py:313
  105.1 11.9 %collective-permute-start.11 = (bf16[64,1024]{1,0:T(8,128)(2,1)S(1)}, bf16[64,1024]{1,0:T(8,128)(2,1)S(1)}, u32[]{:S(2)}, u32[]{:S(2)}) collective-permute-start(bf16[64,1024]{1,0:T(8,128)(2,1)S(1)} %collective-permute-done.10.refs_6_), channel_id=1, source_target_pairs={{0,1},{1,0},{2,3},{3,2},{4,5},{5,4},{6,7},{7,6},{8,9},{9,8},{10,11... | collective-permute-start | bytes 393224 | tf_op jit(solution)/shard_map/ppermute | solution.py:313
  105.6 1.0 copy-start.9
  105.6 11.3 %collective-permute-start.7 = (bf16[64,1024]{1,0:T(8,128)(2,1)S(1)}, bf16[64,1024]{1,0:T(8,128)(2,1)S(1)}, u32[]{:S(2)}, u32[]{:S(2)}) collective-permute-start(bf16[64,1024]{1,0:T(8,128)(2,1)S(1)} %collective-permute-done.6.refs_2_), channel_id=1, source_target_pairs={{0,1},{1,0},{2,3},{3,2},{4,5},{5,4},{6,7},{7,6},{8,9},{9,8},{10,11... | collective-permute-start | bytes 393224 | tf_op jit(solution)/shard_map/ppermute | solution.py:313
  105.7 1.2 copy-start.10
  105.7 11.3 %collective-permute-start.9 = (bf16[64,1024]{1,0:T(8,128)(2,1)S(1)}, bf16[64,1024]{1,0:T(8,128)(2,1)S(1)}, u32[]{:S(2)}, u32[]{:S(2)}) collective-permute-start(bf16[64,1024]{1,0:T(8,128)(2,1)S(1)} %collective-permute-done.8.refs_4_), channel_id=1, source_target_pairs={{0,1},{1,0},{2,3},{3,2},{4,5},{5,4},{6,7},{7,6},{8,9},{9,8},{10,11... | collective-permute-start | bytes 393224 | tf_op jit(solution)/shard_map/ppermute | solution.py:313
  107.0 1.0 copy-start.11
  116.0 1.0 copy-start.7

commit v2 on v1

--- a/solution.py
+++ b/solution.py
@@ -109,7 +109,7 @@
 BF16 = jnp.bfloat16
 
 
-def call(kernel, outs, operands, scalars=0, scratch=(), limit=48, flops=0):
+def call(kernel, outs, operands, scalars=0, scratch=(), limit=32, flops=0):
     smem = pl.BlockSpec(memory_space=pltpu.SMEM)
     vmem = pl.BlockSpec(memory_space=pltpu.VMEM)
     in_specs = [smem] * scalars + [vmem] * (len(operands) - scalars)
@@ -141,61 +141,61 @@
     return (column == lanes).astype(F32).astype(BF16)
 
 
-def pick_kernel(row_ref, replay_ref, out_ref):
+def pick_kernel(row_ref, owner_ref, goal_ref, replay_ref, out_ref, state_ref):
     rows = row_ref.shape[1]
     wide = jnp.broadcast_to(row_ref[...].astype(F32), (8, rows))
     column = wide.T[:, 0:1].astype(jnp.int32)
-    out_ref[...] = dot(one_hot(column, replay_ref.shape[0]), replay_ref[...]).astype(BF16)
+    picked = dot(one_hot(column, replay_ref.shape[0]), replay_ref[...]).astype(BF16)
+    state_ref[...] = picked
+    out_ref[0:rows, :] = picked
+    shape = (out_ref.shape[0] - rows, rows)
+    lines = lax.broadcasted_iota(jnp.int32, shape, 0)
+    goal = goal_ref[...]
+    code = jnp.where(lines == 0, owner_ref[...], jnp.where(lines == 1, goal >> 7, goal & 127))
+    out_ref[rows:, :] = jnp.zeros((shape[0], out_ref.shape[1]), BF16)
+    out_ref[rows:, 0:rows] = code.astype(F32).astype(BF16)
 
 
 def found_kernel(shards, slots, here_ref, *refs):
-    wants, replay_ref, out_ref, hits_ref = refs[:shards], refs[shards], refs[-2], refs[-1]
+    wants, replay_ref = refs[:shards], refs[shards]
+    outs, all_ref, hits_ref = refs[shards + 1 : -2], refs[-2], refs[-1]
     here = here_ref[0]
-    rows = wants[0].shape[1]
+    rows = hits_ref.shape[1]
     hits_ref[...] = jnp.zeros_like(hits_ref)
+    codes = [want[rows:, 0:rows].astype(F32) for want in wants]
+    owned = [code[0:1, :].astype(jnp.int32) == here for code in codes]
     for step in range(shards):
-        hits_ref[step : step + 1, :] = (wants[step][0:1, :] == here).astype(F32)
+        hits_ref[step : step + 1, :] = owned[step].astype(F32)
     before = dot(hits_ref[...].astype(BF16), below(rows))
     places = lax.broadcasted_iota(jnp.int32, (slots, rows), 0)
     for step in range(shards):
-        rank = before[step : step + 1, :].astype(jnp.int32)
-        chosen = (places == rank) & (wants[step][0:1, :] == here)
-        asked = jnp.where(chosen, wants[step][1:2, :].astype(F32), 0.0)
-        column = jnp.sum(asked, axis=1, keepdims=True).astype(jnp.int32)
+        chosen = (places == before[step : step + 1, :].astype(jnp.int32)) & owned[step]
+        goal = codes[step][1:2, :] * 128.0 + codes[step][2:3, :]
+        column = jnp.sum(jnp.where(chosen, goal, 0.0), axis=1, keepdims=True).astype(jnp.int32)
         hot = one_hot(column, replay_ref.shape[0])
-        out_ref[step * slots : (step + 1) * slots, :] = dot(hot, replay_ref[...]).astype(BF16)
-
-
-def place_kernel(shards, slots, here_ref, *refs):
-    wants, out_ref, place_ref = refs[:shards], refs[-2], refs[-1]
-    here = here_ref[0]
-    rows = wants[0].shape[1]
-    tri = below(rows)
-    place_ref[...] = jnp.zeros_like(place_ref)
-    owners = lax.broadcasted_iota(jnp.int32, (place_ref.shape[0], rows), 0)
+        outs[step][...] = dot(hot, replay_ref[...]).astype(BF16)
     for step in range(shards):
-        owner = wants[step][0:1, :]
-        hits = (owners == owner).astype(F32)
-        rank = jnp.sum(dot(hits.astype(BF16), tri) * hits, axis=0, keepdims=True)
-        turn = here - owner
-        turn = jnp.where(turn < 0, turn + shards, turn)
-        block = step - turn
-        block = jnp.where(block < 0, block + shards, block)
-        spot = ((turn * shards + block) * slots).astype(F32) + rank
-        place_ref[step : step + 1, :] = spot
-    out_ref[...] = place_ref[...].T
-
-
-def select_kernel(shards, place_ref, *refs):
-    founds, out_ref = refs[:shards], refs[-1]
-    rows = place_ref.shape[0]
-    size = founds[0].shape[0]
-    for step in range(shards):
-        column = place_ref[:, step : step + 1].astype(jnp.int32)
-        total = dot(one_hot(column, size), founds[0][...])
-        for turn in range(1, shards):
-            total += dot(one_hot(column - turn * size, size), founds[turn][...])
-        out_ref[step * rows : (step + 1) * rows, :] = total.astype(BF16)
+        all_ref[step * rows : (step + 1) * rows, :] = wants[step][0:rows, :]
+
+
+def place_kernel(shards, slots, here_ref, owner_ref, out_ref):
+    rows = owner_ref.shape[1]
+    owner = owner_ref[...]
+    hits = (lax.broadcasted_iota(jnp.int32, (8, rows), 0) == owner).astype(F32)
+    rank = jnp.sum(dot(hits.astype(BF16), below(rows)) * hits, axis=0, keepdims=True)
+    turn = owner - here_ref[0]
+    turn = jnp.where(turn < 0, turn + shards, turn)
+    spot = (turn * slots).astype(F32) + rank
+    column = jnp.broadcast_to(spot, (8, rows)).T[:, 0:1].astype(jnp.int32)
+    out_ref[...] = one_hot(column, shards * slots)
+
+
+def select_kernel(hot_ref, *refs):
+    founds, out_ref, held_ref = refs[:-2], refs[-2], refs[-1]
+    slots = founds[0].shape[0]
+    for turn, found in enumerate(founds):
+        held_ref[turn * slots : (turn + 1) * slots, :] = found[...]
+    out_ref[...] = dot(hot_ref[...], held_ref[...]).astype(BF16)
 
 
 def hidden(group, pieces, first_ref):
@@ -231,38 +231,19 @@
     slope_ref[...] = slope
 
 
-def embed_kernel(group_ref, *refs):
-    pieces, firsts, seconds = refs[:4], refs[4:8], refs[8:12]
-    psi_ref, act_ref, slope_ref, total_ref = refs[12:]
-    group = group_ref[0]
-    for index in range(4):
-        act, slope = slope_of(hidden(group, pieces, firsts[index]))
-        act = act.astype(BF16)
-        if index == 0:
-            act_ref[...] = act
-            slope_ref[...] = slope
-        term = dot(act, seconds[index][...])
-        if index == 0:
-            total_ref[...] = term
-        elif index < 3:
-            total_ref[...] += term
-        else:
-            psi_ref[...] = (total_ref[...] + term).astype(BF16)
-
-
 def grads_kernel(shards, group_ref, here_ref, *refs):
-    halves = refs[: 2 * shards]
-    psi_ref, state_x, goal_x = refs[2 * shards], refs[2 * shards + 1 :][:4], refs[2 * shards + 5 :][:4]
-    rest = refs[2 * shards + 9 :]
-    state_act, state_slope, goal_act, goal_slope, state_second, goal_second = rest[:6]
-    outs, (phi_ref, column_ref, grad_ref) = rest[6:10], rest[10:]
+    halves, refs = (refs[: 2 * shards], refs[2 * shards : 4 * shards]), refs[4 * shards :]
+    state_x, goal_x, refs = refs[:4], refs[4:8], refs[8:]
+    state_act, state_slope, goal_act, goal_slope, state_second, goal_second = refs[:6]
+    outs, (phi_ref, psi_ref, column_ref, grad_ref) = refs[6:10], refs[10:]
     group, here = group_ref[0], here_ref[0]
-    half = halves[0].shape[0]
+    half = halves[0][0].shape[0]
     core = group % 2
-    for step in range(shards):
-        for other in range(2):
-            start = step * 2 * half + (core ^ other) * half
-            phi_ref[pl.ds(pl.multiple_of(start, half), half), :] = halves[2 * step + other][...]
+    for pieces, whole_ref in zip(halves, (phi_ref, psi_ref)):
+        for step in range(shards):
+            for other in range(2):
+                start = step * 2 * half + (core ^ other) * half
+                whole_ref[pl.ds(pl.multiple_of(start, half), half), :] = pieces[2 * step + other][...]
     batch, width = phi_ref.shape
     scale = 4.0 / math.sqrt(width)
     scores = scale * dot(phi_ref[...], psi_ref[...], ((1,), (1,)))
@@ -305,88 +286,95 @@
     units, embed = state_second.shape
     batch = shards * rows
 
+    def turn(array, step):
+        return lax.ppermute(array, "dp", [(i, (i + step) % shards) for i in range(shards)])
+
     def around(array):
-        turns = [[(i, (i + s) % shards) for i in range(shards)] for s in range(1, shards)]
-        return [array] + [lax.ppermute(array, "dp", turn) for turn in turns]
+        return [array] + [turn(array, step) for step in range(1, shards)]
 
     def swap(array, bit):
         return lax.ppermute(array, "mp", [(i, i ^ bit) for i in range(4)])
 
-    want = jnp.concatenate([goal_owner.reshape(1, rows), goal_row.reshape(1, rows)], axis=0)
-    wants = around(want)
-    (state_mine,) = call(
-        pick_kernel, [((rows, width), BF16)], [sa_row.reshape(1, rows), replay], flops=2 * rows * replay.size
-    )
-    state_near = [state_mine] + [swap(state_mine, bit) for bit in (1, 2, 3)]
-    firsts = [goal_first, swap(goal_first, 1), swap(goal_first, 2)]
-    seconds = [goal_second, swap(goal_second, 1), swap(goal_second, 2)]
-    firsts.append(swap(firsts[2], 1))
-    seconds.append(swap(seconds[2], 1))
-    (found,) = call(
+    def near(array):
+        return [array] + [swap(array, bit) for bit in (1, 2, 3)]
+
+    def chip_wide(array):
+        across = swap(array, 2)
+        return [array, swap(array, 1), across, swap(across, 1)]
+
+    def embed_rows(pieces, first, second):
+        keep, send = call(
+            part_kernel,
+            [((rows // 2, embed), F32), ((rows // 2, embed), F32)],
+            [group, *pieces, first, second],
+            scalars=1,
+            scratch=[pltpu.VMEM((rows, embed), F32)],
+            flops=4 * rows * first.size,
+        )
+        chip = keep + swap(send, 1)
+        half = (chip + swap(chip, 2)).astype(BF16)
+        halves = []
+        for piece in around(half):
+            halves += [piece, swap(piece, 1)]
+        return halves
+
+    def hidden_rows(pieces, first):
+        return call(
+            act_kernel,
+            [((batch, units), BF16), ((batch, units), F32)],
+            [group, *pieces, first],
+            scalars=1,
+            flops=2 * batch * first.size,
+        )
+
+    owner = goal_owner.reshape(1, rows)
+    carried, state_mine = call(
+        pick_kernel,
+        [((rows + 16, width), BF16), ((rows, width), BF16)],
+        [sa_row.reshape(1, rows), owner, goal_row.reshape(1, rows), replay],
+        flops=2 * rows * replay.size,
+    )
+    wants = around(carried)
+    state_near = near(state_mine)
+    *founds, state_all = call(
         functools.partial(found_kernel, shards, slots),
-        [((shards * slots, width), BF16)],
+        [((slots, width), BF16)] * shards + [((batch, width), BF16)],
         [here, *wants, replay],
         scalars=1,
         scratch=[pltpu.VMEM((8, rows), F32)],
         flops=2 * shards * slots * replay.size,
     )
-    founds = around(found)
-    (places,) = call(
+    founds = [founds[0]] + [turn(founds[step], shards - step) for step in range(1, shards)]
+    (hot,) = call(
         functools.partial(place_kernel, shards, slots),
-        [((rows, 8), F32)],
-        [here, *wants],
+        [((rows, shards * slots), BF16)],
+        [here, owner],
         scalars=1,
-        scratch=[pltpu.VMEM((8, rows), F32)],
-    )
-    keep, send = call(
-        part_kernel,
-        [((rows // 2, embed), F32), ((rows // 2, embed), F32)],
-        [group, *state_near, state_first, state_second],
-        scalars=1,
-        scratch=[pltpu.VMEM((rows, embed), F32)],
-        flops=4 * rows * state_first.size,
-    )
-    chip = keep + swap(send, 1)
-    phi_half = (chip + swap(chip, 2)).astype(BF16)
-    phi_halves = []
-    for piece in around(phi_half):
-        phi_halves += [piece, swap(piece, 1)]
-    state_all = jnp.concatenate(around(state_mine), axis=0)
-    state_x = [state_all, swap(state_all, 1), swap(state_all, 2)]
-    state_x.append(swap(state_x[2], 1))
-    state_act, state_slope = call(
-        act_kernel,
-        [((batch, units), BF16), ((batch, units), F32)],
-        [group, *state_x, state_first],
-        scalars=1,
-        flops=2 * batch * state_first.size,
-    )
-    (goal_all,) = call(
-        functools.partial(select_kernel, shards),
-        [((batch, width), BF16)],
-        [places, *founds],
-        flops=2 * batch * shards * found.size,
-    )
-    goal_x = [goal_all, swap(goal_all, 1), swap(goal_all, 2)]
-    goal_x.append(swap(goal_x[2], 1))
-    psi, goal_act, goal_slope = call(
-        embed_kernel,
-        [((batch, embed), BF16), ((batch, units), BF16), ((batch, units), F32)],
-        [group, *goal_x, *firsts, *seconds],
-        scalars=1,
-        scratch=[pltpu.VMEM((batch, embed), F32)],
-        flops=16 * batch * goal_first.size,
-    )
+    )
+    phi = embed_rows(state_near, state_first, state_second)
+    (goal_mine,) = call(
+        select_kernel,
+        [((rows, width), BF16)],
+        [hot, *founds],
+        scratch=[pltpu.VMEM((shards * slots, width), BF16)],
+    )
+    psi = embed_rows(near(goal_mine), goal_first, goal_second)
+    goal_all = jnp.concatenate(around(goal_mine), axis=0)
+    state_x = chip_wide(state_all)
+    goal_x = chip_wide(goal_all)
+    state_act, state_slope = hidden_rows(state_x, state_first)
+    goal_act, goal_slope = hidden_rows(goal_x, goal_first)
     latents = 4 * width // shards
     outs = [((latents, units), F32), ((units, embed // shards), F32)]
     return tuple(
         call(
             functools.partial(grads_kernel, shards),
             outs + outs,
-            [group, here, *phi_halves, psi, *state_x, *goal_x]
+            [group, here, *phi, *psi, *state_x, *goal_x]
             + [state_act, state_slope, goal_act, goal_slope, state_second, goal_second],
             scalars=2,
             scratch=[
+                pltpu.VMEM((batch, embed), BF16),
                 pltpu.VMEM((batch, embed), BF16),
                 pltpu.VMEM((batch, width), BF16),
                 pltpu.VMEM((batch, embed), BF16),

time: 125 us -> 92.2 us (0.74)
  waiting for transfers between devices: 67.6 us -> 38.6 us
  Pallas kernels: 19.3 us -> 10.5 us
  starting transfers between devices: 28.5 us -> 36.3 us
  local copies, waits for them, and re-layouts: 7.74 us -> 5.52 us
    ppermute x21 -> x24, waiting for transfers between devices: 35.5 us -> 11.3 us  [swap(): return lax.ppermute(array, 'mp', [(i, i ^ bit) for i in range(4)])]
    ppermute x12 -> x15, starting transfers between devices: 16.1 us -> 25 us  [turn(): lax.ppermute(array, 'dp', [(i, (i + step) % shards) for i in range(shards)])]
    pallas_call x8 -> x9, Pallas kernels: 19.3 us -> 10.5 us  [call(): pl.pallas_call(kernel, out_shape=[jax.ShapeDtypeStruct(s, d) for s, d in...]
    ppermute x12 -> x15, waiting for transfers between devices: 32.1 us -> 27.3 us  [turn(): lax.ppermute(array, 'dp', [(i, (i + step) % shards) for i in range(shards)])]
    unnamed x24 -> x22, local copies, waits for them, and re-layouts: 7.74 us -> 5.52 us
    ppermute x21 -> x24, starting transfers between devices: 12.4 us -> 11.3 us  [swap(): return lax.ppermute(array, 'mp', [(i, i ^ bit) for i in range(4)])]
  transfers between devices with their start and end apart: 33 -> 39, of which waited for: 13 -> 11; matrix products, arithmetic and copies ran while one was open for 1% -> 0% of each run, Pallas kernels for 9% -> 4%
where the time goes in v2:
time: 92.2 us; the launch traced here: 92 us
  waiting for transfers between devices  38.6 us (42%)
  starting transfers between devices  36.3 us (39%)
  Pallas kernels  10.5 us (11%)
  local copies, waits for them, and re-layouts  5.52 us (6%)
    ppermute x15, waiting for transfers between devices, turn(): lax.ppermute(array, 'dp', [(i, (i + step) % shards) for i in range(shards)])  27.3 us
    ppermute x15, starting transfers between devices, turn(): lax.ppermute(array, 'dp', [(i, (i + step) % shards) for i in range(shards)])  25 us
    ppermute x24, waiting for transfers between devices, swap(): return lax.ppermute(array, 'mp', [(i, i ^ bit) for i in range(4)])  11.3 us
    ppermute x24, starting transfers between devices, swap(): return lax.ppermute(array, 'mp', [(i, i ^ bit) for i in range(4)])  11.3 us
    pallas_call x9, Pallas kernels, call(): pl.pallas_call(kernel, out_shape=[jax.ShapeDtypeStruct(s, d) for s, d in...  10.5 us
    unnamed x22, local copies, waits for them, and re-layouts  5.52 us
  transfers between devices with their start and end apart: 39, of which 11 were waited for; matrix products, arithmetic and copies ran while one was open for 0% of the time, Pallas kernels for 4%

profile of v2, /device:TPU:0, one launch (start us, length us, event | category | flops | bytes accessed | tf_op | source)
XLA Modules:
  0.0 92.0 jit_solution(916005573181156503)
XLA Ops:
  0.6 0.0 copy-start.2
  0.7 1.1 %copy-done.2 = bf16[1024,256]{1,0:T(8,128)(2,1)S(1)} copy-done((bf16[1024,256]{1,0:T(8,128)(2,1)S(1)}, bf16[1024,256]{1,0:T(8,128)(2,1)}, u32[]{:S(2)}) %copy-start.2) | copy-done | bytes 524312
  1.8 0.7 copy-done.7
  2.4 0.7 copy-done.9
  3.1 0.7 copy-done.10
  3.7 0.3 shard_map.111
  4.1 5.1 %collective-permute-start.14 = (bf16[144,256]{1,0:T(8,128)(2,1)S(1)}, bf16[144,256]{1,0:T(8,128)(2,1)S(1)}, u32[]{:S(2)}, u32[]{:S(2)}) collective-permute-start(bf16[144,256]{1,0:T(8,128)(2,1)S(1)} %get-tuple-element.22.refs_0_), channel_id=1, source_target_pairs={{0,12},{4,0},{8,4},{12,8},{1,13},{5,1},{9,5},{13,9},{2,14},{6,2},{... | collective-permute-start | bytes 221192 | tf_op jit(solution)/shard_map/ppermute | solution.py:290
  9.2 0.0 collective-permute-start.13
  9.2 1.0 %collective-permute-start.12 = (bf16[144,256]{1,0:T(8,128)(2,1)S(1)}, bf16[144,256]{1,0:T(8,128)(2,1)S(1)}, u32[]{:S(2)}, u32[]{:S(2)}) collective-permute-start(bf16[144,256]{1,0:T(8,128)(2,1)S(1)} %get-tuple-element.22.refs_0_), channel_id=1, source_target_pairs={{0,4},{4,8},{8,12},{12,0},{1,5},{5,9},{9,13},{13,1},{2,6},{6,10},{... | collective-permute-start | bytes 221192 | tf_op jit(solution)/shard_map/ppermute | solution.py:290
  10.2 1.7 %collective-permute-done.14.refs_3_ = bf16[144,256]{1,0:T(8,128)(2,1)S(1)} collective-permute-done((bf16[144,256]{1,0:T(8,128)(2,1)S(1)}, bf16[144,256]{1,0:T(8,128)(2,1)S(1)}, u32[]{:S(2)}, u32[]{:S(2)}) %collective-permute-start.14) | collective-permute-done | bytes 73760 | tf_op jit(solution)/shard_map/ppermute | solution.py:290
  11.9 4.3 %collective-permute-done.13.refs_2_ = bf16[144,256]{1,0:T(8,128)(2,1)S(1)} collective-permute-done((bf16[144,256]{1,0:T(8,128)(2,1)S(1)}, bf16[144,256]{1,0:T(8,128)(2,1)S(1)}, u32[]{:S(2)}, u32[]{:S(2)}) %collective-permute-start.13) | collective-permute-done | bytes 73760 | tf_op jit(solution)/shard_map/ppermute | solution.py:290
  16.2 1.0 %copy-done.3 = bf16[1024,256]{1,0:T(8,128)(2,1)S(1)} copy-done((bf16[1024,256]{1,0:T(8,128)(2,1)S(1)}, bf16[1024,256]{1,0:T(8,128)(2,1)}, u32[]{:S(2)}) %copy-start.3) | copy-done | bytes 524312
  17.2 0.7 shard_map.114
  18.0 2.0 %collective-permute-start.15 = (bf16[64,256]{1,0:T(8,128)(2,1)S(1)}, bf16[64,256]{1,0:T(8,128)(2,1)S(1)}, u32[]{:S(2)}, u32[]{:S(2)}) collective-permute-start(bf16[64,256]{1,0:T(8,128)(2,1)S(1)} %get-tuple-element.24), channel_id=1, source_target_pairs={{0,12},{4,0},{8,4},{12,8},{1,13},{5,1},{9,5},{13,9},{2,14},{6,2},{... | collective-permute-start | bytes 98312 | tf_op jit(solution)/shard_map/ppermute | solution.py:290
  20.0 1.5 %collective-permute-start.1 = (bf16[128,256]{1,0:T(8,128)(2,1)S(1)}, bf16[128,256]{1,0:T(8,128)(2,1)S(1)}, u32[]{:S(2)}, u32[]{:S(2)}) collective-permute-start(bf16[128,256]{1,0:T(8,128)(2,1)S(1)} %get-tuple-element.19.refs_0_), channel_id=1, source_target_pairs={{0,2},{1,3},{2,0},{3,1},{4,6},{5,7},{6,4},{7,5},{8,10},{9,11},{10,... | collective-permute-start | bytes 196616 | tf_op jit(solution)/shard_map/ppermute | solution.py:296
  21.5 0.3 collective-permute-start
  21.9 0.0 collective-permute-start.16
  21.9 0.1 collective-permute-done.15.refs_1_
  21.9 1.9 %collective-permute-start.17 = (bf16[64,256]{1,0:T(8,128)(2,1)S(1)}, bf16[64,256]{1,0:T(8,128)(2,1)S(1)}, u32[]{:S(2)}, u32[]{:S(2)}) collective-permute-start(bf16[64,256]{1,0:T(8,128)(2,1)S(1)} %get-tuple-element.26), channel_id=1, source_target_pairs={{0,4},{4,8},{8,12},{12,0},{1,5},{5,9},{9,13},{13,1},{2,6},{6,10},{... | collective-permute-start | bytes 98312 | tf_op jit(solution)/shard_map/ppermute | solution.py:290
  23.8 0.3 shard_map.113.hot_ref
  24.1 2.9 %collective-permute-done.16.refs_2_ = bf16[64,256]{1,0:T(8,128)(2,1)S(1)} collective-permute-done((bf16[64,256]{1,0:T(8,128)(2,1)S(1)}, bf16[64,256]{1,0:T(8,128)(2,1)S(1)}, u32[]{:S(2)}, u32[]{:S(2)}) %collective-permute-start.16) | collective-permute-done | bytes 32800 | tf_op jit(solution)/shard_map/ppermute | solution.py:290
  27.0 0.6 collective-permute-done.17.refs_3_
  27.6 0.2 shard_map.115.refs_0_
  27.8 0.1 collective-permute-start.20
  27.9 1.5 %collective-permute-start.19 = (bf16[128,256]{1,0:T(8,128)(2,1)S(1)}, bf16[128,256]{1,0:T(8,128)(2,1)S(1)}, u32[]{:S(2)}, u32[]{:S(2)}) collective-permute-start(bf16[128,256]{1,0:T(8,128)(2,1)S(1)} %shard_map.115.refs_0_), channel_id=1, source_target_pairs={{0,2},{1,3},{2,0},{3,1},{4,6},{5,7},{6,4},{7,5},{8,10},{9,11},{10,... | collective-permute-start | bytes 196616 | tf_op jit(solution)/shard_map/ppermute | solution.py:296
  29.4 0.0 collective-permute-done.2.refs_3_
  29.4 0.0 collective-permute-done.1.refs_2_
  29.4 0.0 collective-permute-done.refs_1_
  29.5 0.0 copy-start.4
  29.5 1.2 %copy-done.4 = bf16[512,1024]{1,0:T(8,128)(2,1)S(1)} copy-done((bf16[512,1024]{1,0:T(8,128)(2,1)S(1)}, bf16[512,1024]{1,0:T(8,128)(2,1)}, u32[]{:S(2)}) %copy-start.4) | copy-done | bytes 1048600
  30.7 0.6 shard_map.112
  31.3 0.4 collective-permute-start.3
  31.7 0.2 collective-permute-start.18
  31.9 2.0 %collective-permute-start.35 = (bf16[128,256]{1,0:T(8,128)(2,1)S(1)}, bf16[128,256]{1,0:T(8,128)(2,1)S(1)}, u32[]{:S(2)}, u32[]{:S(2)}) collective-permute-start(bf16[128,256]{1,0:T(8,128)(2,1)S(1)} %shard_map.115.refs_0_), channel_id=1, source_target_pairs={{0,12},{4,0},{8,4},{12,8},{1,13},{5,1},{9,5},{13,9},{2,14},{6,2},{... | collective-permute-start | bytes 196616 | tf_op jit(solution)/shard_map/ppermute | solution.py:290
  33.9 1.1 %collective-permute-start.33 = (bf16[128,256]{1,0:T(8,128)(2,1)S(1)}, bf16[128,256]{1,0:T(8,128)(2,1)S(1)}, u32[]{:S(2)}, u32[]{:S(2)}) collective-permute-start(bf16[128,256]{1,0:T(8,128)(2,1)S(1)} %shard_map.115.refs_0_), channel_id=1, source_target_pairs={{0,4},{4,8},{8,12},{12,0},{1,5},{5,9},{9,13},{13,1},{2,6},{6,10},{... | collective-permute-start | bytes 196616 | tf_op jit(solution)/shard_map/ppermute | solution.py:290
  35.0 1.4 %collective-permute-start.31 = (bf16[512,256]{1,0:T(8,128)(2,1)S(1)}, bf16[512,256]{1,0:T(8,128)(2,1)S(1)}, u32[]{:S(2)}, u32[]{:S(2)}) collective-permute-start(bf16[512,256]{1,0:T(8,128)(2,1)S(1)} %get-tuple-element.29.refs_0_.refs_16_), channel_id=1, source_target_pairs={{0,2},{1,3},{2,0},{3,1},{4,6},{5,7},{6,4},{7,5},{8,10},{9,11},{10,... | collective-permute-start | bytes 786440 | tf_op jit(solution)/shard_map/ppermute | solution.py:296
  36.4 0.6 shard_map.116
  37.1 0.1 collective-permute-start.21
  37.1 4.0 %collective-permute-done.34 = bf16[128,256]{1,0:T(8,128)(2,1)S(1)} collective-permute-done((bf16[128,256]{1,0:T(8,128)(2,1)S(1)}, bf16[128,256]{1,0:T(8,128)(2,1)S(1)}, u32[]{:S(2)}, u32[]{:S(2)}) %collective-permute-start.34) | collective-permute-done | bytes 65568 | tf_op jit(solution)/shard_map/ppermute | solution.py:290
  41.1 1.6 %collective-permute-start.37 = (bf16[512,256]{1,0:T(8,128)(2,1)S(1)}, bf16[512,256]{1,0:T(8,128)(2,1)S(1)}, u32[]{:S(2)}, u32[]{:S(2)}) collective-permute-start(bf16[512,256]{1,0:T(8,128)(2,1)S(1)} %pad_maximum_fusion.refs_0_.refs_20_), channel_id=1, source_target_pairs={{0,2},{1,3},{2,0},{3,1},{4,6},{5,7},{6,4},{7,5},{8,10},{9,11},{10,... | collective-permute-start | bytes 786440 | tf_op jit(solution)/shard_map/ppermute | solution.py:296
  42.8 0.6 collective-permute-start.4
  43.3 0.5 collective-permute-start.36
  43.8 0.1 collective-permute-start.32
  44.0 6.4 %collective-permute-done.37.refs_2_.refs_22_ = bf16[512,256]{1,0:T(8,128)(2,1)S(1)} collective-permute-done((bf16[512,256]{1,0:T(8,128)(2,1)S(1)}, bf16[512,256]{1,0:T(8,128)(2,1)S(1)}, u32[]{:S(2)}, u32[]{:S(2)}) %collective-permute-start.37) | collective-permute-done | bytes 262176 | tf_op jit(solution)/shard_map/ppermute | solution.py:296
  50.4 1.5 %collective-permute-start.22 = (f32[64,1024]{1,0:T(8,128)S(1)}, f32[64,1024]{1,0:T(8,128)S(1)}, u32[]{:S(2)}, u32[]{:S(2)}) collective-permute-start(f32[64,1024]{1,0:T(8,128)S(1)} %add.14), channel_id=1, source_target_pairs={{0,2},{1,3},{2,0},{3,1},{4,6},{5,7},{6,4},{7,5},{8,10},{9,11},{10,... | collective-permute-start | bytes 786440 | tf_op jit(solution)/shard_map/ppermute | solution.py:296
  51.9 4.1 %collective-permute-done.4 = f32[64,1024]{1,0:T(8,128)S(1)} collective-permute-done((f32[64,1024]{1,0:T(8,128)S(1)}, f32[64,1024]{1,0:T(8,128)S(1)}, u32[]{:S(2)}, u32[]{:S(2)}) %collective-permute-start.4) | collective-permute-done | bytes 262176 | tf_op jit(solution)/shard_map/ppermute | solution.py:296
  56.0 2.3 %collective-permute-start.10 = (bf16[64,1024]{1,0:T(8,128)(2,1)S(1)}, bf16[64,1024]{1,0:T(8,128)(2,1)S(1)}, u32[]{:S(2)}, u32[]{:S(2)}) collective-permute-start(bf16[64,1024]{1,0:T(8,128)(2,1)S(1)} %add_convert_fusion.1.refs_0_), channel_id=1, source_target_pairs={{0,12},{4,0},{8,4},{12,8},{1,13},{5,1},{9,5},{13,9},{2,14},{6,2},{... | collective-permute-start | bytes 393224 | tf_op jit(solution)/shard_map/ppermute | solution.py:290
  58.4 1.1 %collective-permute-start.8 = (bf16[64,1024]{1,0:T(8,128)(2,1)S(1)}, bf16[64,1024]{1,0:T(8,128)(2,1)S(1)}, u32[]{:S(2)}, u32[]{:S(2)}) collective-permute-start(bf16[64,1024]{1,0:T(8,128)(2,1)S(1)} %add_convert_fusion.1.refs_0_), channel_id=1, source_target_pairs={{0,8},{4,12},{8,0},{12,4},{1,9},{5,13},{9,1},{13,5},{2,10},{6,14},... | collective-permute-start | bytes 393224 | tf_op jit(solution)/shard_map/ppermute | solution.py:290
  59.5 0.3 collective-permute-start.6
  59.8 0.7 collective-permute-done.22
  60.5 2.9 %collective-permute-start.28 = (bf16[64,1024]{1,0:T(8,128)(2,1)S(1)}, bf16[64,1024]{1,0:T(8,128)(2,1)S(1)}, u32[]{:S(2)}, u32[]{:S(2)}) collective-permute-start(bf16[64,1024]{1,0:T(8,128)(2,1)S(1)} %add_convert_fusion.refs_8_), channel_id=1, source_target_pairs={{0,12},{4,0},{8,4},{12,8},{1,13},{5,1},{9,5},{13,9},{2,14},{6,2},{... | collective-permute-start | bytes 393224 | tf_op jit(solution)/shard_map/ppermute | solution.py:290
  63.4 5.3 %collective-permute-start.26 = (bf16[64,1024]{1,0:T(8,128)(2,1)S(1)}, bf16[64,1024]{1,0:T(8,128)(2,1)S(1)}, u32[]{:S(2)}, u32[]{:S(2)}) collective-permute-start(bf16[64,1024]{1,0:T(8,128)(2,1)S(1)} %add_convert_fusion.refs_8_), channel_id=1, source_target_pairs={{0,8},{4,12},{8,0},{12,4},{1,9},{5,13},{9,1},{13,5},{2,10},{6,14},... | collective-permute-start | bytes 393224 | tf_op jit(solution)/shard_map/ppermute | solution.py:290
  68.7 4.9 %collective-permute-done.8.refs_4_ = bf16[64,1024]{1,0:T(8,128)(2,1)S(1)} collective-permute-done((bf16[64,1024]{1,0:T(8,128)(2,1)S(1)}, bf16[64,1024]{1,0:T(8,128)(2,1)S(1)}, u32[]{:S(2)}, u32[]{:S(2)}) %collective-permute-start.8) | collective-permute-done | bytes 131104 | tf_op jit(solution)/shard_map/ppermute | solution.py:290
  73.6 0.5 collective-permute-start.11
  74.1 0.1 collective-permute-start.9
  74.2 8.8 %collective-permute-done.26.refs_12_ = bf16[64,1024]{1,0:T(8,128)(2,1)S(1)} collective-permute-done((bf16[64,1024]{1,0:T(8,128)(2,1)S(1)}, bf16[64,1024]{1,0:T(8,128)(2,1)S(1)}, u32[]{:S(2)}, u32[]{:S(2)}) %collective-permute-start.26) | collective-permute-done | bytes 131104 | tf_op jit(solution)/shard_map/ppermute | solution.py:290
  83.1 0.5 collective-permute-start.29
  83.6 0.1 collective-permute-start.27
  83.6 0.4 collective-permute-start.25
  84.1 1.0 %shard_map.117 = (bf16[512,512]{1,0:T(8,128)(2,1)S(1)}, f32[512,512]{1,0:T(8,128)S(1)}) custom-call(s32[1]{0:T(128)} %bitcast.group_ref, bf16[512,256]{1,0:T(8,128)(2,1)S(1)} %get-tuple-element.29.refs_0_.refs_16_, bf16[512,256]{1,0:T(8,128)(2,1)S(1)} %collective-permute-done.30.refs_1_.refs_17_, ...), custom_call_target="tpu_custom_call" | custom-call | flops 536870912 | bytes 3670020 | tf_op jit(solution)/shard_map/pallas_call | solution.py:118
  85.1 0.0 copy-start.5
  85.1 1.0 %shard_map.118 = (bf16[512,512]{1,0:T(8,128)(2,1)S(1)}, f32[512,512]{1,0:T(8,128)S(1)}) custom-call(s32[1]{0:T(128)} %bitcast.group_ref, bf16[512,256]{1,0:T(8,128)(2,1)S(1)} %pad_maximum_fusion.refs_0_.refs_20_, bf16[512,256]{1,0:T(8,128)(2,1)S(1)} %collective-permute-done.36.refs_1_.refs_21_, ...), custom_call_target="tpu_custom_call" | custom-call | flops 536870912 | bytes 3670020 | tf_op jit(solution)/shard_map/pallas_call | solution.py:118
  86.2 0.2 copy-done.5
  86.3 5.6 %shard_map.119 = (f32[256,512]{1,0:T(8,128)}, f32[512,256]{1,0:T(8,128)}, f32[256,512]{1,0:T(8,128)}, f32[512,256]{1,0:T(8,128)}) custom-call(s32[1]{0:T(128)} %bitcast.group_ref, s32[1]{0:T(128)} %bitcast.1.here_ref, bf16[64,1024]{1,0:T(8,128)(2,1)S(1)} %add_convert_fusion.1.refs_0_, bf16[64,1024]{1,0:T(8,128)(2,1)S(1)} %collective-permute-done.5.refs_1_, ...), custom_call_target="tpu_custom_call" | custom-call | flops 3221225472 | bytes 11534344 | tf_op jit(solution)/shard_map/pallas_call | solution.py:118
  (50 shorter events, 0.3 us)
Async XLA Ops:
  0.6 28.8 %copy-start = (bf16[1024,512]{1,0:T(8,128)(2,1)S(1)}, bf16[1024,512]{1,0:T(8,128)(2,1)}, u32[]{:S(2)}) copy-start(bf16[1024,512]{1,0:T(8,128)(2,1)} %refs_4_.8) | copy-start | bytes 3145732
  0.6 1.1 %copy-start.2 = (bf16[1024,256]{1,0:T(8,128)(2,1)S(1)}, bf16[1024,256]{1,0:T(8,128)(2,1)}, u32[]{:S(2)}) copy-start(bf16[1024,256]{1,0:T(8,128)(2,1)} %refs_4_.6) | copy-start | bytes 1572868
  1.8 0.7 copy-start.7
  2.4 0.7 copy-start.9
  3.1 0.7 copy-start.10
  4.1 7.8 %collective-permute-start.14 = (bf16[144,256]{1,0:T(8,128)(2,1)S(1)}, bf16[144,256]{1,0:T(8,128)(2,1)S(1)}, u32[]{:S(2)}, u32[]{:S(2)}) collective-permute-start(bf16[144,256]{1,0:T(8,128)(2,1)S(1)} %get-tuple-element.22.refs_0_), channel_id=1, source_target_pairs={{0,12},{4,0},{8,4},{12,8},{1,13},{5,1},{9,5},{13,9},{2,14},{6,2},{... | collective-permute-start | bytes 221192 | tf_op jit(solution)/shard_map/ppermute | solution.py:290
  9.2 7.0 %collective-permute-start.13 = (bf16[144,256]{1,0:T(8,128)(2,1)S(1)}, bf16[144,256]{1,0:T(8,128)(2,1)S(1)}, u32[]{:S(2)}, u32[]{:S(2)}) collective-permute-start(bf16[144,256]{1,0:T(8,128)(2,1)S(1)} %get-tuple-element.22.refs_0_), channel_id=1, source_target_pairs={{0,8},{4,12},{8,0},{12,4},{1,9},{5,13},{9,1},{13,5},{2,10},{6,14},... | collective-permute-start | bytes 221192 | tf_op jit(solution)/shard_map/ppermute | solution.py:290
  9.2 7.0 %collective-permute-start.12 = (bf16[144,256]{1,0:T(8,128)(2,1)S(1)}, bf16[144,256]{1,0:T(8,128)(2,1)S(1)}, u32[]{:S(2)}, u32[]{:S(2)}) collective-permute-start(bf16[144,256]{1,0:T(8,128)(2,1)S(1)} %get-tuple-element.22.refs_0_), channel_id=1, source_target_pairs={{0,4},{4,8},{8,12},{12,0},{1,5},{5,9},{9,13},{13,1},{2,6},{6,10},{... | collective-permute-start | bytes 221192 | tf_op jit(solution)/shard_map/ppermute | solution.py:290
  16.2 1.0 %copy-start.3 = (bf16[1024,256]{1,0:T(8,128)(2,1)S(1)}, bf16[1024,256]{1,0:T(8,128)(2,1)}, u32[]{:S(2)}) copy-start(bf16[1024,256]{1,0:T(8,128)(2,1)} %refs_4_.6) | copy-start | bytes 1572868
  18.0 4.0 %collective-permute-start.15 = (bf16[64,256]{1,0:T(8,128)(2,1)S(1)}, bf16[64,256]{1,0:T(8,128)(2,1)S(1)}, u32[]{:S(2)}, u32[]{:S(2)}) collective-permute-start(bf16[64,256]{1,0:T(8,128)(2,1)S(1)} %get-tuple-element.24), channel_id=1, source_target_pairs={{0,12},{4,0},{8,4},{12,8},{1,13},{5,1},{9,5},{13,9},{2,14},{6,2},{... | collective-permute-start | bytes 98312 | tf_op jit(solution)/shard_map/ppermute | solution.py:290
  20.0 9.4 %collective-permute-start.2 = (bf16[128,256]{1,0:T(8,128)(2,1)S(1)}, bf16[128,256]{1,0:T(8,128)(2,1)S(1)}, u32[]{:S(2)}, u32[]{:S(2)}) collective-permute-start(bf16[128,256]{1,0:T(8,128)(2,1)S(1)} %get-tuple-element.19.refs_0_), channel_id=1, source_target_pairs={{0,3},{1,2},{2,1},{3,0},{4,7},{5,6},{6,5},{7,4},{8,11},{9,10},{10,... | collective-permute-start | bytes 196616 | tf_op jit(solution)/shard_map/ppermute | solution.py:296
  20.0 9.4 %collective-permute-start.1 = (bf16[128,256]{1,0:T(8,128)(2,1)S(1)}, bf16[128,256]{1,0:T(8,128)(2,1)S(1)}, u32[]{:S(2)}, u32[]{:S(2)}) collective-permute-start(bf16[128,256]{1,0:T(8,128)(2,1)S(1)} %get-tuple-element.19.refs_0_), channel_id=1, source_target_pairs={{0,2},{1,3},{2,0},{3,1},{4,6},{5,7},{6,4},{7,5},{8,10},{9,11},{10,... | collective-permute-start | bytes 196616 | tf_op jit(solution)/shard_map/ppermute | solution.py:296
  21.5 7.9 %collective-permute-start = (bf16[128,256]{1,0:T(8,128)(2,1)S(1)}, bf16[128,256]{1,0:T(8,128)(2,1)S(1)}, u32[]{:S(2)}, u32[]{:S(2)}) collective-permute-start(bf16[128,256]{1,0:T(8,128)(2,1)S(1)} %get-tuple-element.19.refs_0_), channel_id=1, source_target_pairs={{0,1},{1,0},{2,3},{3,2},{4,5},{5,4},{6,7},{7,6},{8,9},{9,8},{10,11... | collective-permute-start | bytes 196616 | tf_op jit(solution)/shard_map/ppermute | solution.py:296
  21.9 5.2 %collective-permute-start.16 = (bf16[64,256]{1,0:T(8,128)(2,1)S(1)}, bf16[64,256]{1,0:T(8,128)(2,1)S(1)}, u32[]{:S(2)}, u32[]{:S(2)}) collective-permute-start(bf16[64,256]{1,0:T(8,128)(2,1)S(1)} %get-tuple-element.25), channel_id=1, source_target_pairs={{0,8},{4,12},{8,0},{12,4},{1,9},{5,13},{9,1},{13,5},{2,10},{6,14},... | collective-permute-start | bytes 98312 | tf_op jit(solution)/shard_map/ppermute | solution.py:290
  21.9 1.9 %copy-start.8 = (s32[128,1]{0,1:T(1,128)S(1)}, s32[128,1]{0,1:T(1,128)}, u32[]{:S(2)}) copy-start(s32[128,1]{0,1:T(1,128)} %param.10) | copy-start | bytes 1540
  21.9 5.7 %collective-permute-start.17 = (bf16[64,256]{1,0:T(8,128)(2,1)S(1)}, bf16[64,256]{1,0:T(8,128)(2,1)S(1)}, u32[]{:S(2)}, u32[]{:S(2)}) collective-permute-start(bf16[64,256]{1,0:T(8,128)(2,1)S(1)} %get-tuple-element.26), channel_id=1, source_target_pairs={{0,4},{4,8},{8,12},{12,0},{1,5},{5,9},{9,13},{13,1},{2,6},{6,10},{... | collective-permute-start | bytes 98312 | tf_op jit(solution)/shard_map/ppermute | solution.py:290
  27.8 6.1 %collective-permute-start.20 = (bf16[128,256]{1,0:T(8,128)(2,1)S(1)}, bf16[128,256]{1,0:T(8,128)(2,1)S(1)}, u32[]{:S(2)}, u32[]{:S(2)}) collective-permute-start(bf16[128,256]{1,0:T(8,128)(2,1)S(1)} %shard_map.115.refs_0_), channel_id=1, source_target_pairs={{0,3},{1,2},{2,1},{3,0},{4,7},{5,6},{6,5},{7,4},{8,11},{9,10},{10,... | collective-permute-start | bytes 196616 | tf_op jit(solution)/shard_map/ppermute | solution.py:296
  27.9 6.0 %collective-permute-start.19 = (bf16[128,256]{1,0:T(8,128)(2,1)S(1)}, bf16[128,256]{1,0:T(8,128)(2,1)S(1)}, u32[]{:S(2)}, u32[]{:S(2)}) collective-permute-start(bf16[128,256]{1,0:T(8,128)(2,1)S(1)} %shard_map.115.refs_0_), channel_id=1, source_target_pairs={{0,2},{1,3},{2,0},{3,1},{4,6},{5,7},{6,4},{7,5},{8,10},{9,11},{10,... | collective-permute-start | bytes 196616 | tf_op jit(solution)/shard_map/ppermute | solution.py:296
  29.5 1.2 %copy-start.4 = (bf16[512,1024]{1,0:T(8,128)(2,1)S(1)}, bf16[512,1024]{1,0:T(8,128)(2,1)}, u32[]{:S(2)}) copy-start(bf16[512,1024]{1,0:T(8,128)(2,1)} %refs_28_.1) | copy-start | bytes 3145732
  30.7 5.7 %copy-start.1 = (bf16[1024,512]{1,0:T(8,128)(2,1)S(1)}, bf16[1024,512]{1,0:T(8,128)(2,1)}, u32[]{:S(2)}) copy-start(bf16[1024,512]{1,0:T(8,128)(2,1)} %refs_4_.9) | copy-start | bytes 3145732
  30.7 5.7 %copy-start.6 = (bf16[512,1024]{1,0:T(8,128)(2,1)S(1)}, bf16[512,1024]{1,0:T(8,128)(2,1)}, u32[]{:S(2)}) copy-start(bf16[512,1024]{1,0:T(8,128)(2,1)} %refs_29_.1) | copy-start | bytes 3145732
  31.3 11.4 %collective-permute-start.3 = (f32[64,1024]{1,0:T(8,128)S(1)}, f32[64,1024]{1,0:T(8,128)S(1)}, u32[]{:S(2)}, u32[]{:S(2)}) collective-permute-start(f32[64,1024]{1,0:T(8,128)S(1)} %get-tuple-element.21), channel_id=1, source_target_pairs={{0,1},{1,0},{2,3},{3,2},{4,5},{5,4},{6,7},{7,6},{8,9},{9,8},{10,11... | collective-permute-start | bytes 786440 | tf_op jit(solution)/shard_map/ppermute | solution.py:296
  31.7 3.3 %collective-permute-start.18 = (bf16[128,256]{1,0:T(8,128)(2,1)S(1)}, bf16[128,256]{1,0:T(8,128)(2,1)S(1)}, u32[]{:S(2)}, u32[]{:S(2)}) collective-permute-start(bf16[128,256]{1,0:T(8,128)(2,1)S(1)} %shard_map.115.refs_0_), channel_id=1, source_target_pairs={{0,1},{1,0},{2,3},{3,2},{4,5},{5,4},{6,7},{7,6},{8,9},{9,8},{10,11... | collective-permute-start | bytes 196616 | tf_op jit(solution)/shard_map/ppermute | solution.py:296
  31.9 5.1 %collective-permute-start.35 = (bf16[128,256]{1,0:T(8,128)(2,1)S(1)}, bf16[128,256]{1,0:T(8,128)(2,1)S(1)}, u32[]{:S(2)}, u32[]{:S(2)}) collective-permute-start(bf16[128,256]{1,0:T(8,128)(2,1)S(1)} %shard_map.115.refs_0_), channel_id=1, source_target_pairs={{0,12},{4,0},{8,4},{12,8},{1,13},{5,1},{9,5},{13,9},{2,14},{6,2},{... | collective-permute-start | bytes 196616 | tf_op jit(solution)/shard_map/ppermute | solution.py:290
  33.9 7.2 %collective-permute-start.34 = (bf16[128,256]{1,0:T(8,128)(2,1)S(1)}, bf16[128,256]{1,0:T(8,128)(2,1)S(1)}, u32[]{:S(2)}, u32[]{:S(2)}) collective-permute-start(bf16[128,256]{1,0:T(8,128)(2,1)S(1)} %shard_map.115.refs_0_), channel_id=1, source_target_pairs={{0,8},{4,12},{8,0},{12,4},{1,9},{5,13},{9,1},{13,5},{2,10},{6,14},... | collective-permute-start | bytes 196616 | tf_op jit(solution)/shard_map/ppermute | solution.py:290
  33.9 7.2 %collective-permute-start.33 = (bf16[128,256]{1,0:T(8,128)(2,1)S(1)}, bf16[128,256]{1,0:T(8,128)(2,1)S(1)}, u32[]{:S(2)}, u32[]{:S(2)}) collective-permute-start(bf16[128,256]{1,0:T(8,128)(2,1)S(1)} %shard_map.115.refs_0_), channel_id=1, source_target_pairs={{0,4},{4,8},{8,12},{12,0},{1,5},{5,9},{9,13},{13,1},{2,6},{6,10},{... | collective-permute-start | bytes 196616 | tf_op jit(solution)/shard_map/ppermute | solution.py:290
  35.0 8.3 %collective-permute-start.31 = (bf16[512,256]{1,0:T(8,128)(2,1)S(1)}, bf16[512,256]{1,0:T(8,128)(2,1)S(1)}, u32[]{:S(2)}, u32[]{:S(2)}) collective-permute-start(bf16[512,256]{1,0:T(8,128)(2,1)S(1)} %get-tuple-element.29.refs_0_.refs_16_), channel_id=1, source_target_pairs={{0,2},{1,3},{2,0},{3,1},{4,6},{5,7},{6,4},{7,5},{8,10},{9,11},{10,... | collective-permute-start | bytes 786440 | tf_op jit(solution)/shard_map/ppermute | solution.py:296
  37.1 6.8 %collective-permute-start.21 = (f32[64,1024]{1,0:T(8,128)S(1)}, f32[64,1024]{1,0:T(8,128)S(1)}, u32[]{:S(2)}, u32[]{:S(2)}) collective-permute-start(f32[64,1024]{1,0:T(8,128)S(1)} %get-tuple-element.28), channel_id=1, source_target_pairs={{0,1},{1,0},{2,3},{3,2},{4,5},{5,4},{6,7},{7,6},{8,9},{9,8},{10,11... | collective-permute-start | bytes 786440 | tf_op jit(solution)/shard_map/ppermute | solution.py:296
  41.1 9.3 %collective-permute-start.37 = (bf16[512,256]{1,0:T(8,128)(2,1)S(1)}, bf16[512,256]{1,0:T(8,128)(2,1)S(1)}, u32[]{:S(2)}, u32[]{:S(2)}) collective-permute-start(bf16[512,256]{1,0:T(8,128)(2,1)S(1)} %pad_maximum_fusion.refs_0_.refs_20_), channel_id=1, source_target_pairs={{0,2},{1,3},{2,0},{3,1},{4,6},{5,7},{6,4},{7,5},{8,10},{9,11},{10,... | collective-permute-start | bytes 786440 | tf_op jit(solution)/shard_map/ppermute | solution.py:296
  42.8 13.2 %collective-permute-start.4 = (f32[64,1024]{1,0:T(8,128)S(1)}, f32[64,1024]{1,0:T(8,128)S(1)}, u32[]{:S(2)}, u32[]{:S(2)}) collective-permute-start(f32[64,1024]{1,0:T(8,128)S(1)} %add.12), channel_id=1, source_target_pairs={{0,2},{1,3},{2,0},{3,1},{4,6},{5,7},{6,4},{7,5},{8,10},{9,11},{10,... | collective-permute-start | bytes 786440 | tf_op jit(solution)/shard_map/ppermute | solution.py:296
  43.3 12.7 %collective-permute-start.30 = (bf16[512,256]{1,0:T(8,128)(2,1)S(1)}, bf16[512,256]{1,0:T(8,128)(2,1)S(1)}, u32[]{:S(2)}, u32[]{:S(2)}) collective-permute-start(bf16[512,256]{1,0:T(8,128)(2,1)S(1)} %get-tuple-element.29.refs_0_.refs_16_), channel_id=1, source_target_pairs={{0,1},{1,0},{2,3},{3,2},{4,5},{5,4},{6,7},{7,6},{8,9},{9,8},{10,11... | collective-permute-start | bytes 786440 | tf_op jit(solution)/shard_map/ppermute | solution.py:296
  43.3 15.0 %collective-permute-start.36 = (bf16[512,256]{1,0:T(8,128)(2,1)S(1)}, bf16[512,256]{1,0:T(8,128)(2,1)S(1)}, u32[]{:S(2)}, u32[]{:S(2)}) collective-permute-start(bf16[512,256]{1,0:T(8,128)(2,1)S(1)} %pad_maximum_fusion.refs_0_.refs_20_), channel_id=1, source_target_pairs={{0,1},{1,0},{2,3},{3,2},{4,5},{5,4},{6,7},{7,6},{8,9},{9,8},{10,11... | collective-permute-start | bytes 786440 | tf_op jit(solution)/shard_map/ppermute | solution.py:296
  43.8 15.6 %collective-permute-start.32 = (bf16[512,256]{1,0:T(8,128)(2,1)S(1)}, bf16[512,256]{1,0:T(8,128)(2,1)S(1)}, u32[]{:S(2)}, u32[]{:S(2)}) collective-permute-start(bf16[512,256]{1,0:T(8,128)(2,1)S(1)} %collective-permute-done.31.refs_2_.refs_18_), channel_id=1, source_target_pairs={{0,1},{1,0},{2,3},{3,2},{4,5},{5,4},{6,7},{7,6},{8,9},{9,8},{10,11... | collective-permute-start | bytes 786440 | tf_op jit(solution)/shard_map/ppermute | solution.py:296
  50.4 10.1 %collective-permute-start.22 = (f32[64,1024]{1,0:T(8,128)S(1)}, f32[64,1024]{1,0:T(8,128)S(1)}, u32[]{:S(2)}, u32[]{:S(2)}) collective-permute-start(f32[64,1024]{1,0:T(8,128)S(1)} %add.14), channel_id=1, source_target_pairs={{0,2},{1,3},{2,0},{3,1},{4,6},{5,7},{6,4},{7,5},{8,10},{9,11},{10,... | collective-permute-start | bytes 786440 | tf_op jit(solution)/shard_map/ppermute | solution.py:296
  56.0 4.5 %collective-permute-start.38 = (bf16[512,256]{1,0:T(8,128)(2,1)S(1)}, bf16[512,256]{1,0:T(8,128)(2,1)S(1)}, u32[]{:S(2)}, u32[]{:S(2)}) collective-permute-start(bf16[512,256]{1,0:T(8,128)(2,1)S(1)} %collective-permute-done.37.refs_2_.refs_22_), channel_id=1, source_target_pairs={{0,1},{1,0},{2,3},{3,2},{4,5},{5,4},{6,7},{7,6},{8,9},{9,8},{10,11... | collective-permute-start | bytes 786440 | tf_op jit(solution)/shard_map/ppermute | solution.py:296
  56.0 7.4 %collective-permute-start.10 = (bf16[64,1024]{1,0:T(8,128)(2,1)S(1)}, bf16[64,1024]{1,0:T(8,128)(2,1)S(1)}, u32[]{:S(2)}, u32[]{:S(2)}) collective-permute-start(bf16[64,1024]{1,0:T(8,128)(2,1)S(1)} %add_convert_fusion.1.refs_0_), channel_id=1, source_target_pairs={{0,12},{4,0},{8,4},{12,8},{1,13},{5,1},{9,5},{13,9},{2,14},{6,2},{... | collective-permute-start | bytes 393224 | tf_op jit(solution)/shard_map/ppermute | solution.py:290
  58.4 15.2 %collective-permute-start.8 = (bf16[64,1024]{1,0:T(8,128)(2,1)S(1)}, bf16[64,1024]{1,0:T(8,128)(2,1)S(1)}, u32[]{:S(2)}, u32[]{:S(2)}) collective-permute-start(bf16[64,1024]{1,0:T(8,128)(2,1)S(1)} %add_convert_fusion.1.refs_0_), channel_id=1, source_target_pairs={{0,8},{4,12},{8,0},{12,4},{1,9},{5,13},{9,1},{13,5},{2,10},{6,14},... | collective-permute-start | bytes 393224 | tf_op jit(solution)/shard_map/ppermute | solution.py:290
  59.5 14.1 %collective-permute-start.6 = (bf16[64,1024]{1,0:T(8,128)(2,1)S(1)}, bf16[64,1024]{1,0:T(8,128)(2,1)S(1)}, u32[]{:S(2)}, u32[]{:S(2)}) collective-permute-start(bf16[64,1024]{1,0:T(8,128)(2,1)S(1)} %add_convert_fusion.1.refs_0_), channel_id=1, source_target_pairs={{0,4},{4,8},{8,12},{12,0},{1,5},{5,9},{9,13},{13,1},{2,6},{6,10},{... | collective-permute-start | bytes 393224 | tf_op jit(solution)/shard_map/ppermute | solution.py:290
  60.5 13.1 %collective-permute-start.5 = (bf16[64,1024]{1,0:T(8,128)(2,1)S(1)}, bf16[64,1024]{1,0:T(8,128)(2,1)S(1)}, u32[]{:S(2)}, u32[]{:S(2)}) collective-permute-start(bf16[64,1024]{1,0:T(8,128)(2,1)S(1)} %add_convert_fusion.1.refs_0_), channel_id=1, source_target_pairs={{0,1},{1,0},{2,3},{3,2},{4,5},{5,4},{6,7},{7,6},{8,9},{9,8},{10,11... | collective-permute-start | bytes 393224 | tf_op jit(solution)/shard_map/ppermute | solution.py:296
  60.5 13.6 %collective-permute-start.28 = (bf16[64,1024]{1,0:T(8,128)(2,1)S(1)}, bf16[64,1024]{1,0:T(8,128)(2,1)S(1)}, u32[]{:S(2)}, u32[]{:S(2)}) collective-permute-start(bf16[64,1024]{1,0:T(8,128)(2,1)S(1)} %add_convert_fusion.refs_8_), channel_id=1, source_target_pairs={{0,12},{4,0},{8,4},{12,8},{1,13},{5,1},{9,5},{13,9},{2,14},{6,2},{... | collective-permute-start | bytes 393224 | tf_op jit(solution)/shard_map/ppermute | solution.py:290
  63.4 19.6 %collective-permute-start.26 = (bf16[64,1024]{1,0:T(8,128)(2,1)S(1)}, bf16[64,1024]{1,0:T(8,128)(2,1)S(1)}, u32[]{:S(2)}, u32[]{:S(2)}) collective-permute-start(bf16[64,1024]{1,0:T(8,128)(2,1)S(1)} %add_convert_fusion.refs_8_), channel_id=1, source_target_pairs={{0,8},{4,12},{8,0},{12,4},{1,9},{5,13},{9,1},{13,5},{2,10},{6,14},... | collective-permute-start | bytes 393224 | tf_op jit(solution)/shard_map/ppermute | solution.py:290
  73.6 9.5 %collective-permute-start.24 = (bf16[64,1024]{1,0:T(8,128)(2,1)S(1)}, bf16[64,1024]{1,0:T(8,128)(2,1)S(1)}, u32[]{:S(2)}, u32[]{:S(2)}) collective-permute-start(bf16[64,1024]{1,0:T(8,128)(2,1)S(1)} %add_convert_fusion.refs_8_), channel_id=1, source_target_pairs={{0,4},{4,8},{8,12},{12,0},{1,5},{5,9},{9,13},{13,1},{2,6},{6,10},{... | collective-permute-start | bytes 393224 | tf_op jit(solution)/shard_map/ppermute | solution.py:290
  73.6 10.0 %collective-permute-start.23 = (bf16[64,1024]{1,0:T(8,128)(2,1)S(1)}, bf16[64,1024]{1,0:T(8,128)(2,1)S(1)}, u32[]{:S(2)}, u32[]{:S(2)}) collective-permute-start(bf16[64,1024]{1,0:T(8,128)(2,1)S(1)} %add_convert_fusion.refs_8_), channel_id=1, source_target_pairs={{0,1},{1,0},{2,3},{3,2},{4,5},{5,4},{6,7},{7,6},{8,9},{9,8},{10,11... | collective-permute-start | bytes 393224 | tf_op jit(solution)/shard_map/ppermute | solution.py:296
  73.6 10.0 %collective-permute-start.11 = (bf16[64,1024]{1,0:T(8,128)(2,1)S(1)}, bf16[64,1024]{1,0:T(8,128)(2,1)S(1)}, u32[]{:S(2)}, u32[]{:S(2)}) collective-permute-start(bf16[64,1024]{1,0:T(8,128)(2,1)S(1)} %collective-permute-done.10.refs_6_), channel_id=1, source_target_pairs={{0,1},{1,0},{2,3},{3,2},{4,5},{5,4},{6,7},{7,6},{8,9},{9,8},{10,11... | collective-permute-start | bytes 393224 | tf_op jit(solution)/shard_map/ppermute | solution.py:296
  74.1 12.0 %collective-permute-start.9 = (bf16[64,1024]{1,0:T(8,128)(2,1)S(1)}, bf16[64,1024]{1,0:T(8,128)(2,1)S(1)}, u32[]{:S(2)}, u32[]{:S(2)}) collective-permute-start(bf16[64,1024]{1,0:T(8,128)(2,1)S(1)} %collective-permute-done.8.refs_4_), channel_id=1, source_target_pairs={{0,1},{1,0},{2,3},{3,2},{4,5},{5,4},{6,7},{7,6},{8,9},{9,8},{10,11... | collective-permute-start | bytes 393224 | tf_op jit(solution)/shard_map/ppermute | solution.py:296
  83.0 3.1 %collective-permute-start.7 = (bf16[64,1024]{1,0:T(8,128)(2,1)S(1)}, bf16[64,1024]{1,0:T(8,128)(2,1)S(1)}, u32[]{:S(2)}, u32[]{:S(2)}) collective-permute-start(bf16[64,1024]{1,0:T(8,128)(2,1)S(1)} %collective-permute-done.6.refs_2_), channel_id=1, source_target_pairs={{0,1},{1,0},{2,3},{3,2},{4,5},{5,4},{6,7},{7,6},{8,9},{9,8},{10,11... | collective-permute-start | bytes 393224 | tf_op jit(solution)/shard_map/ppermute | solution.py:296
  83.1 3.1 %collective-permute-start.29 = (bf16[64,1024]{1,0:T(8,128)(2,1)S(1)}, bf16[64,1024]{1,0:T(8,128)(2,1)S(1)}, u32[]{:S(2)}, u32[]{:S(2)}) collective-permute-start(bf16[64,1024]{1,0:T(8,128)(2,1)S(1)} %collective-permute-done.28.refs_14_), channel_id=1, source_target_pairs={{0,1},{1,0},{2,3},{3,2},{4,5},{5,4},{6,7},{7,6},{8,9},{9,8},{10,11... | collective-permute-start | bytes 393224 | tf_op jit(solution)/shard_map/ppermute | solution.py:296
  83.6 2.6 %collective-permute-start.27 = (bf16[64,1024]{1,0:T(8,128)(2,1)S(1)}, bf16[64,1024]{1,0:T(8,128)(2,1)S(1)}, u32[]{:S(2)}, u32[]{:S(2)}) collective-permute-start(bf16[64,1024]{1,0:T(8,128)(2,1)S(1)} %collective-permute-done.26.refs_12_), channel_id=1, source_target_pairs={{0,1},{1,0},{2,3},{3,2},{4,5},{5,4},{6,7},{7,6},{8,9},{9,8},{10,11... | collective-permute-start | bytes 393224 | tf_op jit(solution)/shard_map/ppermute | solution.py:296
  83.6 2.5 %collective-permute-start.25 = (bf16[64,1024]{1,0:T(8,128)(2,1)S(1)}, bf16[64,1024]{1,0:T(8,128)(2,1)S(1)}, u32[]{:S(2)}, u32[]{:S(2)}) collective-permute-start(bf16[64,1024]{1,0:T(8,128)(2,1)S(1)} %collective-permute-done.24.refs_10_), channel_id=1, source_target_pairs={{0,1},{1,0},{2,3},{3,2},{4,5},{5,4},{6,7},{7,6},{8,9},{9,8},{10,11... | collective-permute-start | bytes 393224 | tf_op jit(solution)/shard_map/ppermute | solution.py:296
  85.1 1.2 %copy-start.5 = (bf16[512,1024]{1,0:T(8,128)(2,1)S(1)}, bf16[512,1024]{1,0:T(8,128)(2,1)}, u32[]{:S(2)}) copy-start(bf16[512,1024]{1,0:T(8,128)(2,1)} %refs_28_.1) | copy-start | bytes 3145732
